TPU v7x, 32 devices: a whole 2x2x4 slice. The times are simulated.
32 devices in a mesh: dom: 8 (over z, x), neu: 4 (over y, core).
Axes of the slice: x: 2, y: 2, z: 4, core: 2. Of those that a mesh axis runs over, the one named last changes fastest.
Arguments:
- state_lower: bfloat16 [2, 3072, 8192], P(None, 'dom', 'neu'), may hold values from -4 to 4
- state_gap: bfloat16 [2, 3072, 8192], P(None, 'dom', 'neu'), may hold values from 0.099609375 to 4
- state_alpha: bfloat16 [2, 3072, 2, 8192], P(None, 'dom', None, 'neu'), may hold values from 0 to 1
- split_beta: bfloat16 [3072, 2], P('dom'), may hold values from 0.0019989014 to 0.029907227
- split_neuron: int32 [3072], P('dom'), may hold values from 0 to 16383
- split_sign: int32 [3072], P('dom'), may hold values 0 or 1
- send_counts: int32 [8, 8], replicated, may hold values from 0 to 48, as said below
- spec_row: bfloat16 [8192], P('neu'), may hold values from -0.0007324219 to 0.0007324219
- weight: bfloat16 [8192, 8192], P('neu', 'dom'), may hold values from -0.09375 to 0.09375
Outputs:
- moved_lower: bfloat16 [2, 1536, 8192], P(None, 'dom', 'neu')
- moved_gap: bfloat16 [2, 1536, 8192], P(None, 'dom', 'neu')
- moved_alpha: bfloat16 [2, 1536, 2, 8192], P(None, 'dom', None, 'neu')
- moved_beta: bfloat16 [1536, 2], P('dom')
- moved_neuron: int32 [1536], P('dom')
- moved_sign: int32 [1536], P('dom')
- bounds: float32 [1536, 2], P('dom')
Inputs may be any that keep to these rules, and one draw needn't show every extreme that they name: send_counts[d, e] subdomains go from device d to device e of dom; every column sums to 192; the devices fall into pairs, drawn from the seed, whose two counts to any destination add up to 48; some entry equals 48.
All inputs are finite; a program needn't handle non-finite values. No bound on the sum of `split_sign` on one device may be relied on, other than what follows from the above.
Results may differ from a plain program's by a relative error of at most 0.001.
Values may be sent and summed in bfloat16 or wider, within the bound.
No kernel may reach another device: no remote copies, remote signals or barrier semaphores. Data moves between devices by JAX's collectives and lax.ppermute only.
A program may use at most 192 MiB of HBM per device.

v0:
```python
import jax
import jax.numpy as jnp
from jax import lax
from jax.sharding import PartitionSpec as P

WIDTH = 8192
DOM_DEV = 192


def relaxation(
    coeff_in, lower_layer, gap_layer, alpha_layer, beta_rows, neuron_ids, sign_ids, column_ids
):
    lower_f = lower_layer.astype(jnp.float32)
    gap_f = gap_layer.astype(jnp.float32)
    upper_f = lower_f + gap_f
    active = lower_f >= 0.0
    inactive = upper_f <= 0.0
    upper_slope = jnp.where(active, 1.0, jnp.where(inactive, 0.0, upper_f / gap_f))
    intercept = jnp.where(active | inactive, 0.0, -upper_f * lower_f / gap_f)
    lower_slope = jnp.where(
        active[:, None, :],
        1.0,
        jnp.where(inactive[:, None, :], 0.0, alpha_layer.astype(jnp.float32)),
    )
    chosen = neuron_ids[:, None] == column_ids[None, :]
    split_slope = (sign_ids == 1).astype(jnp.float32)
    upper_slope = jnp.where(chosen, split_slope[:, None], upper_slope)
    intercept = jnp.where(chosen, 0.0, intercept)
    lower_slope = jnp.where(chosen[:, None, :], split_slope[:, None, None], lower_slope)
    signed = (2 * sign_ids - 1).astype(jnp.float32)
    penalty = beta_rows.astype(jnp.float32) * signed[:, None]
    positive = jnp.maximum(coeff_in, 0.0)
    negative = jnp.minimum(coeff_in, 0.0)
    result = (
        positive * lower_slope
        + negative * upper_slope[:, None, :]
        - chosen[:, None, :].astype(jnp.float32) * penalty[:, :, None]
    )
    offset = jnp.sum(negative * intercept[:, None, :], axis=-1)
    return (result, offset)


def settle(block, row_index):
    merged = block.reshape((block.shape[0], block.shape[1] * block.shape[2]) + block.shape[3:])
    return jnp.take(merged, row_index, axis=1)


def shards(
    state_lower,
    state_gap,
    state_alpha,
    split_beta,
    split_neuron,
    split_sign,
    send_counts,
    spec_row,
    weight,
):
    groups = lax.axis_size("dom")
    device_pos = lax.axis_index("dom")
    capacity = 2 * DOM_DEV // groups
    domain_count = DOM_DEV
    narrow = state_lower.shape[2]
    outgoing = lax.dynamic_index_in_dim(send_counts, device_pos, 0, keepdims=False)
    incoming = lax.dynamic_index_in_dim(send_counts, device_pos, 1, keepdims=False)
    out_start = jnp.cumsum(outgoing) - outgoing
    slot_pos = jnp.arange(capacity, dtype=jnp.int32)
    send_index = jnp.where(
        slot_pos[None, :] < outgoing[:, None], out_start[:, None] + slot_pos[None, :], 0
    )
    recv_end = jnp.cumsum(incoming)
    recv_start = recv_end - incoming
    out_pos = jnp.arange(domain_count, dtype=jnp.int32)
    source = jnp.sum((recv_end[None, :] <= out_pos[:, None]).astype(jnp.int32), axis=1)
    owners = jnp.arange(groups, dtype=jnp.int32)
    start_at = jnp.sum(
        jnp.where(source[:, None] == owners[None, :], recv_start[None, :], 0), axis=1
    )
    row_index = source * capacity + out_pos - start_at
    tag_pairs = jnp.stack([split_neuron, split_sign], axis=1)
    tags_in = lax.all_to_all(
        jnp.take(tag_pairs, send_index, axis=0), "dom", split_axis=0, concat_axis=0, tiled=True
    )
    moved_tags = jnp.take(tags_in.reshape(groups * capacity, 2), row_index, axis=0)
    beta_out = jnp.take(split_beta, send_index, axis=0)[None]
    lower_in, gap_in, alpha_in, beta_in = (
        lax.all_to_all(
            jnp.take(state_lower, send_index, axis=1),
            "dom",
            split_axis=1,
            concat_axis=1,
            tiled=True,
        ),
        lax.all_to_all(
            jnp.take(state_gap, send_index, axis=1), "dom", split_axis=1, concat_axis=1, tiled=True
        ),
        lax.all_to_all(
            jnp.take(state_alpha, send_index, axis=1),
            "dom",
            split_axis=1,
            concat_axis=1,
            tiled=True,
        ),
        lax.all_to_all(beta_out, "dom", split_axis=1, concat_axis=1, tiled=True),
    )
    lower_all = settle(lower_in, row_index)
    gap_all = settle(gap_in, row_index)
    alpha_all = settle(alpha_in, row_index)
    outer = (lower_all[1], gap_all[1], alpha_all[1])
    moved_beta = settle(beta_in, row_index)[0]
    neuron_ids = moved_tags[:, 0]
    sign_ids = moved_tags[:, 1]
    column_start = lax.axis_index("neu") * narrow
    local_cols = column_start + jnp.arange(narrow, dtype=jnp.int32)
    spec_sign = jnp.array([1.0, -1.0], dtype=jnp.float32)
    coeff_top = jnp.broadcast_to(
        spec_sign[None, :, None] * spec_row.astype(jnp.float32)[None, None, :],
        (domain_count, 2, narrow),
    )
    relaxed_top, offset_top = relaxation(
        coeff_top,
        outer[0],
        outer[1],
        outer[2],
        moved_beta,
        neuron_ids,
        sign_ids,
        local_cols + WIDTH,
    )
    coeff_panel = relaxed_top.astype(jnp.bfloat16).reshape(domain_count * 2, narrow)
    partial_terms = jnp.dot(
        coeff_panel,
        lax.all_gather(weight, "dom", axis=1, tiled=True),
        preferred_element_type=jnp.float32,
    )
    coeff_low = lax.psum_scatter(
        partial_terms.astype(jnp.bfloat16), "neu", scatter_dimension=1, tiled=True
    ).astype(jnp.float32)
    coeff_low = coeff_low.reshape(domain_count, 2, narrow)
    inner = (lower_all[0], gap_all[0], alpha_all[0])
    relaxed_low, offset_low = relaxation(
        coeff_low, inner[0], inner[1], inner[2], moved_beta, neuron_ids, sign_ids, local_cols
    )
    lower_base = inner[0].astype(jnp.float32)
    upper_base = lower_base + inner[1].astype(jnp.float32)
    box_term = jnp.sum(
        jnp.maximum(relaxed_low, 0.0) * lower_base[:, None, :]
        + jnp.minimum(relaxed_low, 0.0) * upper_base[:, None, :],
        axis=-1,
    )
    totals = lax.psum(offset_top + offset_low + box_term, "neu")
    bounds = jnp.stack([totals[:, 0], -totals[:, 1]], axis=1)
    moved_lower = jnp.stack([inner[0], outer[0]])
    moved_gap = jnp.stack([inner[1], outer[1]])
    moved_alpha = jnp.stack([inner[2], outer[2]])
    return (moved_lower, moved_gap, moved_alpha, moved_beta, neuron_ids, sign_ids, bounds)


def solution(mesh):
    in_specs = (
        P(None, "dom", "neu"),
        P(None, "dom", "neu"),
        P(None, "dom", None, "neu"),
        P("dom", None),
        P("dom"),
        P("dom"),
        P(),
        P("neu"),
        P("neu", "dom"),
    )
    out_specs = (
        P(None, "dom", "neu"),
        P(None, "dom", "neu"),
        P(None, "dom", None, "neu"),
        P("dom", None),
        P("dom"),
        P("dom"),
        P("dom", None),
    )
    return jax.shard_map(shards, mesh=mesh, in_specs=in_specs, out_specs=out_specs, check_vma=False)
```

profile of v0, /device:TPU:0, one launch (start us, length us, event | category | flops | bytes accessed | tf_op | source)
XLA Modules:
  0.0 916.9 jit_solution(10194309981466718185)
XLA Ops:
  12.3 7.3 all-to-all-start.3
  21.8 14.3 %gather_fusion.6 = bf16[384,2,2048]{2,0,1:T(8,128)(2,1)} fusion(bf16[2,384,2048]{2,1,0:T(8,128)(2,1)S(1)} %copy-done, s32[1024]{0:T(1024)S(1)} %pad_clamp_fusion.3), kind=kCustom, calls=%fused_computation.clone | custom fusion | bytes 6292992 | tf_op jit(solution)/shard_map/jit(_take)/gather | solution.py:88
  36.1 23.3 %gather_fusion.8 = bf16[384,2,2048]{2,0,1:T(8,128)(2,1)} fusion(bf16[2,384,2048]{2,1,0:T(8,128)(2,1)} %param.15, s32[1024]{0:T(1024)S(1)} %pad_clamp_fusion.3), kind=kCustom, calls=%fused_computation.2.clone | custom fusion | bytes 6292992 | tf_op jit(solution)/shard_map/jit(_take)/gather | solution.py:95
  69.3 107.8 %all_to_all.25 = bf16[2,8,48,2048]{3,2,0,1:T(8,128)(2,1)} all-to-all(bf16[2,8,48,2048]{3,2,0,1:T(8,128)(2,1)S(1)} %get-tuple-element.101), channel_id=1, replica_groups=mesh['dom'=8,'neu'=4] {'dom'}, dimensions={1} | all-to-all | bytes 6291456 | tf_op jit(solution)/shard_map/all_to_all | solution.py:87
  180.9 22.4 %gather_fusion = bf16[384,2,2,2048]{3,2,1,0:T(2,128)(2,1)} fusion(bf16[2,384,2,2048]{3,2,1,0:T(2,128)(2,1)} %param.16, s32[1024]{0:T(1024)S(1)} %pad_clamp_fusion.1), kind=kCustom, calls=%fused_computation.4 | custom fusion | bytes 12584448 | tf_op jit(solution)/shard_map/jit(_take)/gather | solution.py:98
  203.3 6.2 copy.133
  210.3 14.0 %copy.134 = bf16[2,8,48,2,2048]{4,3,2,0,1:T(2,128)(2,1)} copy(bf16[2,8,48,2,2048]{4,2,1,3,0:T(8,128)(2,1)S(1)} %select_bitcast_fusion) | data formatting | bytes 12582912 | tf_op jit(solution)/shard_map/jit(_take)/select_n | solution.py:98
  224.3 52.7 %all-to-all-done.1 = bf16[2,8,48,2048]{3,2,0,1:T(8,128)(2,1)S(1)} async-done(((bf16[2,8,48,2048]{3,2,0,1:T(8,128)(2,1)}), bf16[2,8,48,2048]{3,2,0,1:T(8,128)(2,1)S(1)}, u32[]{:S(2)}, u32[]{:S(2)}) %all-to-all-start.1) | async-done | bytes 3145760 | tf_op jit(solution)/shard_map/all_to_all | solution.py:94
  278.6 32.9 %all-to-all-start.2 = ((bf16[2,8,48,2,2048]{4,3,2,0,1:T(2,128)(2,1)}), bf16[2,8,48,2,2048]{4,3,2,0,1:T(2,128)(2,1)}, u32[]{:S(2)}, u32[]{:S(2)}) async-start(bf16[2,8,48,2,2048]{4,3,2,0,1:T(2,128)(2,1)} %copy.134), calls=%async_computation.2 | async-start | bytes 12582912 | tf_op jit(solution)/shard_map/all_to_all | solution.py:97
  331.0 5.3 broadcast_in_dim.261
  344.3 12.6 %gather_fusion.7 = bf16[192,2,2048]{2,1,0:T(2,128)(2,1)S(1)} fusion(bf16[2,384,2048]{2,0,1:T(2,128)(2,1)} %bitcast.87, s32[1024]{0:T(1024)S(1)} %pad_clamp_fusion.2), kind=kCustom, calls=%fused_computation.1.clone | custom fusion | bytes 3146496 | tf_op jit(solution)/shard_map/jit(_take)/gather | solution.py:45
  365.1 12.6 %gather_fusion.9 = bf16[192,2,2048]{2,1,0:T(2,128)(2,1)} fusion(bf16[2,384,2048]{2,0,1:T(2,128)(2,1)} %bitcast.86, s32[1024]{0:T(1024)S(1)} %pad_clamp_fusion.2), kind=kCustom, calls=%fused_computation.3.clone | custom fusion | bytes 3146496 | tf_op jit(solution)/shard_map/jit(_take)/gather | solution.py:45
  391.1 5.7 mul.193
  400.3 5.3 broadcast_in_dim.269
  409.6 5.3 broadcast_in_dim.266
  414.9 83.6 %all-to-all-done.2 = bf16[2,8,48,2,2048]{4,3,2,0,1:T(2,128)(2,1)} async-done(((bf16[2,8,48,2,2048]{4,3,2,0,1:T(2,128)(2,1)}), bf16[2,8,48,2,2048]{4,3,2,0,1:T(2,128)(2,1)}, u32[]{:S(2)}, u32[]{:S(2)}) %all-to-all-start.2) | async-done | bytes 6291488 | tf_op jit(solution)/shard_map/all_to_all | solution.py:97
  498.5 6.9 copy.135
  505.4 14.2 %gather_fusion.1 = bf16[192,2,2,2048]{3,2,1,0:T(2,128)(2,1)} fusion(bf16[2,384,2,2048]{3,2,1,0:T(2,128)(2,1)} %bitcast.83, s32[1024]{0:T(1024)} %copy-done.23), kind=kCustom, calls=%fused_computation.5 | custom fusion | bytes 6292224 | tf_op jit(solution)/shard_map/jit(_take)/gather | solution.py:45
  519.7 5.0 fusion.8
  524.7 6.3 slice_convert_fusion
  531.0 5.3 reshape.679
  536.3 248.7 %all-gather.2.cloned.1.call-done = bf16[2048,8192]{1,0:T(8,128)(2,1)} async-done(((bf16[2048,1024]{1,0:T(8,128)(2,1)}), bf16[2048,8192]{1,0:T(8,128)(2,1)}) %all-gather.2.cloned.1.call-update) | async-done | bytes 33554448 | tf_op jit(solution)/shard_map/all_gather | solution.py:133
  785.0 29.1 %convolution_convert_fusion = bf16[384,8192]{1,0:T(8,128)(2,1)} fusion(bf16[2048,8192]{1,0:T(8,128)(2,1)} %all-gather.2.cloned.1.call-done, f32[384,2048]{1,0:T(8,128)} %mul.195, f32[384,2048]{1,0:T(8,128)} %mul.193, f32[384,2048]{1,0:T(8,128)} %broadcast_in_dim.259, pred[384,2048]{1,0:T(32,128)(4,1)} %broadcast_in_dim.261, ...), kind=kOutput, calls=%fused_computation.10 | convolution fusion | flops 12894339072 | bytes 54791168 | tf_op jit(solution)/shard_map/dot_general | solution.py:131
  819.0 5.6 mul.212
  828.3 6.1 broadcast_in_dim.277
  842.1 5.4 mul.205
  850.9 5.3 mul.209
  864.6 5.3 mul.218
  878.0 5.4 mul.215
  887.3 5.2 reshape.683
  892.6 9.1 fusion.2
  902.2 6.8 psum.7
  (169 shorter events, 120.8 us)
Async XLA Ops:
  7.2 14.6 %copy-start = (bf16[2,384,2048]{2,1,0:T(8,128)(2,1)S(1)}, bf16[2,384,2048]{2,1,0:T(8,128)(2,1)}, u32[]{:S(2)}) copy-start(bf16[2,384,2048]{2,1,0:T(8,128)(2,1)} %param.14) | copy-start | bytes 9437188
  7.2 12.5 %copy-start.31 = (s32[384]{0:T(512)S(1)}, s32[384]{0:T(512)}, u32[]{:S(2)}) copy-start(s32[384]{0:T(512)} %param.18) | copy-start | bytes 4612
  7.2 12.5 %copy-start.32 = (s32[384]{0:T(512)S(1)}, s32[384]{0:T(512)}, u32[]{:S(2)}) copy-start(s32[384]{0:T(512)} %param.19) | copy-start | bytes 4612
  7.2 777.8 %all-gather.2.cloned.1.call-start = ((), (), s32[]{:S(2)}) async-start(), calls=%async_computation.6 | async-start | bytes 37748736 | tf_op jit(solution)/shard_map/all_gather | solution.py:133
  12.3 47.2 %all-to-all-start.3 = ((bf16[1,8,48,2]{2,3,0,1:T(2,128)(2,1)}), bf16[1,8,48,2]{2,3,0,1:T(2,128)(2,1)S(1)}, u32[]{:S(2)}, u32[]{:S(2)}) async-start(bf16[1,8,48,2]{2,3,0,1:T(2,128)(2,1)} %broadcast_select_fusion.5), calls=%async_computation.3 | async-start | bytes 8192 | tf_op jit(solution)/shard_map/all_to_all | solution.py:104
  59.5 7.7 copy-start.21
  59.5 9.8 %all-to-all-start.4 = ((s32[8,48,2]{1,2,0:T(2,128)}), s32[8,48,2]{1,2,0:T(2,128)S(1)}, u32[]{:S(2)}, u32[]{:S(2)}) async-start(s32[8,48,2]{1,2,0:T(2,128)} %broadcast_select_fusion.4), calls=%async_computation.4 | async-start | bytes 16384 | tf_op jit(solution)/shard_map/all_to_all | solution.py:81
  177.0 99.9 %all-to-all-start.1 = ((bf16[2,8,48,2048]{3,2,0,1:T(8,128)(2,1)}), bf16[2,8,48,2048]{3,2,0,1:T(8,128)(2,1)S(1)}, u32[]{:S(2)}, u32[]{:S(2)}) async-start(bf16[2,8,48,2048]{3,2,0,1:T(8,128)(2,1)} %get-tuple-element.100), calls=%async_computation.1 | async-start | bytes 6291456 | tf_op jit(solution)/shard_map/all_to_all | solution.py:94
  224.3 87.3 %copy-start.27 = (s32[8,8]{1,0:T(8,128)S(1)}, s32[8,8]{1,0:T(8,128)}, u32[]{:S(2)}) copy-start(s32[8,8]{1,0:T(8,128)} %param.20) | copy-start | bytes 772
  224.3 87.6 %copy-start.29 = (bf16[2048]{0:T(1024)(128)(2,1)S(1)}, bf16[2048]{0:T(1024)(128)(2,1)}, u32[]{:S(2)}) copy-start(bf16[2048]{0:T(1024)(128)(2,1)} %param.21) | copy-start | bytes 12292
  224.3 87.6 %copy-start.34 = (f32[2]{0:T(128)S(1)}, f32[2]{0:T(128)}, u32[]{:S(2)}) copy-start(f32[2]{0:T(128)} %constant.140.clone) | copy-start | bytes 28
  278.6 219.9 %all-to-all-start.2 = ((bf16[2,8,48,2,2048]{4,3,2,0,1:T(2,128)(2,1)}), bf16[2,8,48,2,2048]{4,3,2,0,1:T(2,128)(2,1)}, u32[]{:S(2)}, u32[]{:S(2)}) async-start(bf16[2,8,48,2,2048]{4,3,2,0,1:T(2,128)(2,1)} %copy.134), calls=%async_computation.2 | async-start | bytes 12582912 | tf_op jit(solution)/shard_map/all_to_all | solution.py:97
  311.5 581.1 %reduce-scatter.2.cloned.1.call-start = ((), (), s32[]{:S(2)}) async-start(), calls=%async_computation.7 | async-start | bytes 7864320 | tf_op jit(solution)/shard_map/reduce_scatter | solution.py:136
  314.1 4.2 copy-start.22
  318.2 60.5 %copy-start.19 = (pred[192]{0:T(512)(128)(4,1)}, pred[192]{0:T(512)(128)(4,1)S(1)}, u32[]{:S(2)}) copy-start(pred[192]{0:T(512)(128)(4,1)S(1)} %get-tuple-element.79) | copy-start | bytes 580
  320.4 18.1 %copy-start.28 = (s32[192]{0:T(256)}, s32[192]{0:T(256)S(1)}, u32[]{:S(2)}) copy-start(s32[192]{0:T(256)S(1)} %get-tuple-element.69) | copy-start | bytes 2308
  320.5 61.3 %copy-start.17 = (s32[192]{0:T(256)}, s32[192]{0:T(256)S(1)}, u32[]{:S(2)}) copy-start(s32[192]{0:T(256)S(1)} %get-tuple-element.70) | copy-start | bytes 2308
  327.3 12.1 %copy-start.8 = (bf16[2,8,48,2048]{3,2,0,1:T(8,128)(2,1)S(1)}, bf16[2,8,48,2048]{3,2,0,1:T(8,128)(2,1)}, u32[]{:S(2)}) copy-start(bf16[2,8,48,2048]{3,2,0,1:T(8,128)(2,1)} %all_to_all.25) | copy-start | bytes 9437188
  382.7 3.6 copy-start.13
  382.7 3.5 copy-start.16
  505.4 14.2 %copy-start.20 = (pred[192]{0:T(512)(128)(4,1)S(1)}, pred[192]{0:T(512)(128)(4,1)}, u32[]{:S(2)}) copy-start(pred[192]{0:T(512)(128)(4,1)} %copy-done.19) | copy-start | bytes 580
  524.6 6.4 copy-start.2
  531.0 254.0 %copy-start.24 = (f32[384]{0:T(512)S(1)}, f32[384]{0:T(512)}, u32[]{:S(2)}) copy-start(f32[384]{0:T(512)} %reshape.782) | copy-start | bytes 4612
  531.0 254.0 %copy-start.25 = (f32[384]{0:T(512)S(1)}, f32[384]{0:T(512)}, u32[]{:S(2)}) copy-start(f32[384]{0:T(512)} %broadcast_in_dim.263) | copy-start | bytes 4612
  828.3 9.3 %copy-start.18 = (s32[192]{0:T(256)S(1)}, s32[192]{0:T(256)}, u32[]{:S(2)}) copy-start(s32[192]{0:T(256)} %copy-done.17) | copy-start | bytes 2308
  842.1 5.4 copy-start.12
  864.6 5.3 copy-start.14
  869.9 4.7 copy-start.10
  878.0 5.4 copy-start.15
  878.0 5.5 copy-start.3
  887.3 5.2 copy-start.26
  892.6 17.1 %copy-start.1 = (bf16[2,384,2048]{2,1,0:T(8,128)(2,1)S(1)}, bf16[2,384,2048]{2,1,0:T(8,128)(2,1)}, u32[]{:S(2)}) copy-start(bf16[2,384,2048]{2,1,0:T(8,128)(2,1)} %param.14) | copy-start | bytes 9437188
  (9 other events, 20.5 us)
Sparse Core Ops, SparseCore 0:
  9.6 775.3 all-gather.1
  814.2 60.3 reduce-scatter.1
where the time goes:
time: 925 us; the launch traced here: 917 us
  waiting for transfers between devices  388 us (42%)
  local copies, waits for them, and re-layouts  273 us (30%)
  blocking collectives  115 us (12%)
  other arithmetic  49.6 us (5%)
  starting transfers between devices  47.4 us (5%)
  matrix products  29.1 us (3%)
  between operations  15 us (2%)
    all_gather x1, waiting for transfers between devices, shards(): lax.all_gather(weight, 'dom', axis=1, tiled=True)  249 us
    all_to_all x1, blocking collectives, shards(): lax.all_to_all(jnp.take(state_lower, send_index, axis=1), 'dom', split_ax...  108 us
    all_to_all x1, waiting for transfers between devices, shards(): lax.all_to_all(jnp.take(state_alpha, send_index, axis=1), 'dom', split_ax...  83.6 us
    all_to_all x1, waiting for transfers between devices, shards(): lax.all_to_all(jnp.take(state_gap, send_index, axis=1), 'dom', split_axis...  52.7 us
    gather x4, local copies, waits for them, and re-layouts, settle(): return jnp.take(merged, row_index, axis=1)  40.2 us
    all_to_all x1, starting transfers between devices, shards(): lax.all_to_all(jnp.take(state_alpha, send_index, axis=1), 'dom', split_ax...  32.9 us
    dot_general x1, matrix products, shards(): jnp.dot(coeff_panel, lax.all_gather(weight, 'dom', axis=1, tiled=True), p...  29.1 us
    gather x2, local copies, waits for them, and re-layouts, shards(): jnp.take(state_alpha, send_index, axis=1)  28.6 us
  transfers between devices with their start and end apart: 6, of which 4 were waited for; matrix products, arithmetic and copies ran while one was open for 34% of the time, Pallas kernels for 0%

commit v1 on v0

v1 whole, which is shorter than its diff:
```python
import jax
import jax.numpy as jnp
from jax import lax
from jax.sharding import PartitionSpec as P

BF = jnp.bfloat16
F32 = jnp.float32


def bit_reverse(value, bits):
    out = 0
    for b in range(bits):
        out |= ((value >> b) & 1) << (bits - 1 - b)
    return out


def pick(matrix, rows):
    return jnp.dot(matrix, rows, preferred_element_type=F32).astype(BF)


def slopes(lower, gap, chosen, split_slope):
    low = lower.astype(F32)
    wide = gap.astype(F32)
    high = low + wide
    active = low >= 0.0
    inactive = high <= 0.0
    ratio = high / wide
    upper_slope = jnp.where(active, 1.0, jnp.where(inactive, 0.0, ratio))
    intercept = jnp.where(active | inactive, 0.0, -high * low / wide)
    upper_slope = jnp.where(chosen, split_slope, upper_slope)
    intercept = jnp.where(chosen, 0.0, intercept)
    return low, high, active, inactive, upper_slope, intercept


def lower_slope_of(alpha, active, inactive, chosen, split_slope):
    slope = jnp.where(active, 1.0, jnp.where(inactive, 0.0, alpha.astype(F32)))
    return jnp.where(chosen, split_slope, slope)


def shards(
    state_lower,
    state_gap,
    state_alpha,
    split_beta,
    split_neuron,
    split_sign,
    send_counts,
    spec_row,
    weight,
):
    groups = lax.axis_size("dom")
    cores = lax.axis_size("neu")
    near = groups // cores
    bits = cores.bit_length() - 1
    assert near * cores == groups and 1 << bits == cores
    device_pos = lax.axis_index("dom")
    core_pos = lax.axis_index("neu")
    slots = state_lower.shape[1]
    rows = slots // 2
    cap = slots // groups
    narrow = state_lower.shape[2]
    width = narrow * cores

    def swap(value, mask):
        return lax.ppermute(value, "dom", [(d, d ^ mask) for d in range(groups)])

    def swap_core(value, mask):
        return lax.ppermute(value, "neu", [(c, c ^ mask) for c in range(cores)])

    counts = send_counts.astype(jnp.int32)
    partner = device_pos ^ jnp.arange(groups, dtype=jnp.int32)
    outgoing = lax.dynamic_index_in_dim(counts, device_pos, 0, keepdims=False)
    incoming = lax.dynamic_index_in_dim(counts, device_pos, 1, keepdims=False)
    out_start = jnp.cumsum(outgoing) - outgoing
    in_start = jnp.cumsum(incoming) - incoming
    match = partner[:, None] == jnp.arange(groups, dtype=jnp.int32)[None, :]
    out_at = jnp.sum(jnp.where(match, out_start[None, :], 0), axis=1)
    in_at = jnp.sum(jnp.where(match, in_start[None, :], 0), axis=1)
    in_count = jnp.sum(jnp.where(match, incoming[None, :], 0), axis=1)
    place = jnp.arange(cap, dtype=jnp.int32)
    slot_of = (out_at[:, None] + place[None, :]).reshape(groups * cap)
    send_mat = (slot_of[:, None] == jnp.arange(slots, dtype=jnp.int32)[None, :]).astype(BF)
    row_of = jnp.where(
        place[None, :] < in_count[:, None], in_at[:, None] + place[None, :], -1
    ).reshape(groups * cap)
    recv_mat = (jnp.arange(rows, dtype=jnp.int32)[:, None] == row_of[None, :]).astype(BF)

    def exchange(plane):
        packed = pick(send_mat, plane).reshape(groups, cap, plane.shape[1])
        parts = [packed[0]] + [swap(packed[k], k) for k in range(1, groups)]
        return pick(recv_mat, jnp.concatenate(parts, axis=0))

    tags = jnp.concatenate(
        [
            (split_neuron >> 7).astype(BF)[:, None],
            (split_neuron & 127).astype(BF)[:, None],
            split_sign.astype(BF)[:, None],
            split_beta,
            jnp.zeros((slots, 123), BF),
        ],
        axis=1,
    )
    positive_spec = (spec_row >= 0)[None, :]
    first, second = state_alpha[1, :, 0, :], state_alpha[1, :, 1, :]
    used = jnp.where(positive_spec, first, second)
    unused = jnp.where(positive_spec, second, first)

    moved_tags = exchange(tags)
    lower_top = exchange(state_lower[1])
    gap_top = exchange(state_gap[1])
    used_top = exchange(used)

    neuron_ids = moved_tags[:, 0].astype(jnp.int32) * 128 + moved_tags[:, 1].astype(jnp.int32)
    sign_ids = moved_tags[:, 2].astype(jnp.int32)
    moved_beta = moved_tags[:, 3:5]
    split_slope = (sign_ids == 1).astype(F32)[:, None]
    penalty = moved_beta.astype(F32) * (2 * sign_ids - 1).astype(F32)[:, None]
    columns = core_pos * narrow + jnp.arange(narrow, dtype=jnp.int32)

    panel = weight
    step = 1
    while step < near:
        other = swap(panel, step)
        low_side = (device_pos & step) == 0
        panel = jnp.concatenate(
            [jnp.where(low_side, panel, other), jnp.where(low_side, other, panel)], axis=1
        )
        step *= 2

    chosen = neuron_ids[:, None] == (columns + width)[None, :]
    low, high, active, inactive, upper_slope, intercept = slopes(
        lower_top, gap_top, chosen, split_slope
    )
    lower_slope = lower_slope_of(used_top, active, inactive, chosen, split_slope)
    spec = spec_row.astype(F32)[None, :]
    hit = chosen.astype(F32)
    relaxed_top = []
    offset = []
    for s in range(2):
        coeff = spec if s == 0 else -spec
        value = jnp.maximum(coeff, 0.0) * lower_slope + jnp.minimum(coeff, 0.0) * upper_slope
        relaxed_top.append((value - hit * penalty[:, s : s + 1]).astype(BF))
        offset.append(jnp.sum(jnp.minimum(coeff, 0.0) * intercept, axis=1))
    mine = jnp.concatenate(relaxed_top, axis=0)

    held = {0: mine}
    for b in reversed(range(bits)):
        for delta in list(held):
            held[delta | (1 << b)] = swap(held[delta], near << b)
    partial = jnp.stack(
        [jnp.dot(held[d], panel, preferred_element_type=F32) for d in range(cores)]
    )

    for b in range(bits):
        side = (core_pos >> b) & 1
        half = partial.shape[0] // 2
        keep = lax.dynamic_slice_in_dim(partial, side * half, half, 0)
        give = lax.dynamic_slice_in_dim(partial, (1 - side) * half, half, 0)
        partial = keep + swap_core(give.astype(BF), 1 << b).astype(F32)
    route = []
    for o in range(cores):
        for x in range(near):
            for c in range(cores):
                to = o ^ bit_reverse(c, bits)
                route.append(((o * near + x) * cores + c, (to * near + x) * cores + o))
    coeff_low = lax.ppermute(partial[0].astype(BF), ("dom", "neu"), route).astype(F32)

    lower_low = exchange(state_lower[0])
    gap_low = exchange(state_gap[0])
    alpha_low = [exchange(state_alpha[0, :, s, :]) for s in range(2)]
    unused_top = exchange(unused)

    chosen = neuron_ids[:, None] == columns[None, :]
    low, high, active, inactive, upper_slope, intercept = slopes(
        lower_low, gap_low, chosen, split_slope
    )
    hit = chosen.astype(F32)
    for s in range(2):
        coeff = coeff_low[s * rows : (s + 1) * rows]
        lower_slope = lower_slope_of(alpha_low[s], active, inactive, chosen, split_slope)
        negative = jnp.minimum(coeff, 0.0)
        value = jnp.maximum(coeff, 0.0) * lower_slope + negative * upper_slope
        value = value - hit * penalty[:, s : s + 1]
        offset[s] = offset[s] + jnp.sum(
            negative * intercept + jnp.maximum(value, 0.0) * low + jnp.minimum(value, 0.0) * high,
            axis=1,
        )
    totals = lax.psum(jnp.stack(offset, axis=1), "neu")
    bounds = jnp.stack([totals[:, 0], -totals[:, 1]], axis=1)

    alpha_top = [
        jnp.where(positive_spec, used_top, unused_top),
        jnp.where(positive_spec, unused_top, used_top),
    ]
    moved_lower = jnp.stack([lower_low, lower_top])
    moved_gap = jnp.stack([gap_low, gap_top])
    moved_alpha = jnp.stack([jnp.stack(alpha_low, axis=1), jnp.stack(alpha_top, axis=1)])
    return (moved_lower, moved_gap, moved_alpha, moved_beta, neuron_ids, sign_ids, bounds)


def solution(mesh):
    in_specs = (
        P(None, "dom", "neu"),
        P(None, "dom", "neu"),
        P(None, "dom", None, "neu"),
        P("dom", None),
        P("dom"),
        P("dom"),
        P(),
        P("neu"),
        P("neu", "dom"),
    )
    out_specs = (
        P(None, "dom", "neu"),
        P(None, "dom", "neu"),
        P(None, "dom", None, "neu"),
        P("dom", None),
        P("dom"),
        P("dom"),
        P("dom", None),
    )
    return jax.shard_map(shards, mesh=mesh, in_specs=in_specs, out_specs=out_specs, check_vma=False)
```

time: 925 us -> 702 us (0.76)
  local copies, waits for them, and re-layouts: 273 us -> 64.6 us
  blocking collectives: 115 us -> 35.5 us
  waiting for transfers between devices: 388 us -> 438 us
  starting transfers between devices: 47.4 us -> 89.7 us
  other arithmetic: 49.6 us -> 17 us
  matrix products: 29.1 us -> 48.7 us
  between operations: 15 us -> 2.05 us
    ppermute x0 -> x70, waiting for transfers between devices: none -> 438 us  [the longest x67 421 us: swap(): return lax.ppermute(value, 'dom', [(d, d ^ mask) for d in range(groups)])]
    all_gather x1 -> x0, waiting for transfers between devices: 249 us -> none  [shards(): lax.all_gather(weight, 'dom', axis=1, tiled=True)]
    all_to_all x4 -> x0, waiting for transfers between devices: 138 us -> none  [the longest x1 83.6 us: shards(): lax.all_to_all(jnp.take(state_alpha, send_index, axis=1), 'dom', split_ax...]
    gather x13 -> x0, local copies, waits for them, and re-layouts: 110 us -> none  [the longest x4 40.2 us: settle(): return jnp.take(merged, row_index, axis=1)]
    all_to_all x1 -> x0, blocking collectives: 108 us -> none  [shards(): lax.all_to_all(jnp.take(state_lower, send_index, axis=1), 'dom', split_ax...]
    ppermute x0 -> x70, starting transfers between devices: none -> 89.7 us  [the longest x67 85.3 us: swap(): return lax.ppermute(value, 'dom', [(d, d ^ mask) for d in range(groups)])]
    mul x14 -> x0, local copies, waits for them, and re-layouts: 57.4 us -> none  [the longest x4 15.7 us: relaxation(): chosen[:, None, :].astype(jnp.float32) * penalty[:, :, None]]
    broadcast_in_dim x17 -> x4, local copies, waits for them, and re-layouts: 51.4 us -> 0.36 us  [the longest x1 0.12 us: shards(): (split_neuron & 127).astype(BF)[:, None]]
  transfers between devices with their start and end apart: 6 -> 70, of which waited for: 4 -> 45; matrix products, arithmetic and copies ran while one was open for 34% -> 16% of each run, Pallas kernels for 0% -> 0%
where the time goes in v1:
time: 702 us; the launch traced here: 696 us
  waiting for transfers between devices  438 us (62%)
  starting transfers between devices  89.7 us (13%)
  local copies, waits for them, and re-layouts  64.6 us (9%)
  matrix products  48.7 us (7%)
  blocking collectives  35.5 us (5%)
  other arithmetic  17 us (2%)
    ppermute x67, waiting for transfers between devices, swap(): return lax.ppermute(value, 'dom', [(d, d ^ mask) for d in range(groups)])  421 us
    ppermute x67, starting transfers between devices, swap(): return lax.ppermute(value, 'dom', [(d, d ^ mask) for d in range(groups)])  85.3 us
    unnamed x233, local copies, waits for them, and re-layouts  37 us
    psum x1, blocking collectives, shards(): totals = lax.psum(jnp.stack(offset, axis=1), 'neu')  35.5 us
    dot_general x18, matrix products, pick(): return jnp.dot(matrix, rows, preferred_element_type=F32).astype(BF)  33.3 us
    ppermute x2, waiting for transfers between devices, swap_core(): return lax.ppermute(value, 'neu', [(c, c ^ mask) for c in range(cores)])  17.9 us
    dot_general x4, matrix products, shards(): jnp.dot(held[d], panel, preferred_element_type=F32)  15.4 us
  transfers between devices with their start and end apart: 70, of which 45 were waited for; matrix products, arithmetic and copies ran while one was open for 16% of the time, Pallas kernels for 0%

profile of v1, /device:TPU:0, one launch (start us, length us, event | category | flops | bytes accessed | tf_op | source)
XLA Modules:
  0.0 696.0 jit_solution(9882732464726545676)
XLA Ops:
  31.0 9.8 %fusion.65 = (bf16[1,384,1,2048]{3,2,1,0:T(2,128)(2,1)}, bf16[1,384,1,2048]{3,2,1,0:T(2,128)(2,1)S(1)}, bf16[1,384,1,2048]{3,2,1,0:T(2,128)(2,1)S(1)}, bf16[1,384,1,2048]{3,2,1,0:T(2,128)(2,1)S(1)}) fusion(bf16[2,384,2,2048]{3,2,1,0:T(2,128)(2,1)S(1)} %bitcast.76), kind=kLoop, calls=%fused_computation.236 | loop fusion | bytes 12582912 | tf_op jit(solution)/shard_map/slice | solution.py:170
  103.4 11.6 %collective-permute-done.23 = bf16[48,2048]{1,0:T(8,128)(2,1)S(1)} collective-permute-done((bf16[48,2048]{1,0:T(8,128)(2,1)S(1)}, bf16[48,2048]{1,0:T(8,128)(2,1)S(1)}, u32[]{:S(2)}, u32[]{:S(2)}) %collective-permute-start.23) | collective-permute-done | bytes 196640 | tf_op jit(solution)/shard_map/ppermute | solution.py:65
  129.5 7.6 %collective-permute-done.7 = bf16[48,2048]{1,0:T(8,128)(2,1)S(1)} collective-permute-done((bf16[48,2048]{1,0:T(8,128)(2,1)}, bf16[48,2048]{1,0:T(8,128)(2,1)S(1)}, u32[]{:S(2)}, u32[]{:S(2)}) %collective-permute-start.7) | collective-permute-done | bytes 196640 | tf_op jit(solution)/shard_map/ppermute | solution.py:65
  137.7 7.0 %collective-permute-done.8 = bf16[48,2048]{1,0:T(8,128)(2,1)S(1)} collective-permute-done((bf16[48,2048]{1,0:T(8,128)(2,1)S(1)}, bf16[48,2048]{1,0:T(8,128)(2,1)S(1)}, u32[]{:S(2)}, u32[]{:S(2)}) %collective-permute-start.8) | collective-permute-done | bytes 196640 | tf_op jit(solution)/shard_map/ppermute | solution.py:65
  145.0 7.9 %collective-permute-done.9 = bf16[48,2048]{1,0:T(8,128)(2,1)S(1)} collective-permute-done((bf16[48,2048]{1,0:T(8,128)(2,1)S(1)}, bf16[48,2048]{1,0:T(8,128)(2,1)S(1)}, u32[]{:S(2)}, u32[]{:S(2)}) %collective-permute-start.9) | collective-permute-done | bytes 196640 | tf_op jit(solution)/shard_map/ppermute | solution.py:65
  152.9 12.7 %collective-permute-done.10 = bf16[48,2048]{1,0:T(8,128)(2,1)S(1)} collective-permute-done((bf16[48,2048]{1,0:T(8,128)(2,1)S(1)}, bf16[48,2048]{1,0:T(8,128)(2,1)S(1)}, u32[]{:S(2)}, u32[]{:S(2)}) %collective-permute-start.10) | collective-permute-done | bytes 196640 | tf_op jit(solution)/shard_map/ppermute | solution.py:65
  165.6 8.4 %collective-permute-done.11 = bf16[48,2048]{1,0:T(8,128)(2,1)S(1)} collective-permute-done((bf16[48,2048]{1,0:T(8,128)(2,1)S(1)}, bf16[48,2048]{1,0:T(8,128)(2,1)S(1)}, u32[]{:S(2)}, u32[]{:S(2)}) %collective-permute-start.11) | collective-permute-done | bytes 196640 | tf_op jit(solution)/shard_map/ppermute | solution.py:65
  183.7 8.2 %collective-permute-done.13 = bf16[48,2048]{1,0:T(8,128)(2,1)S(1)} collective-permute-done((bf16[48,2048]{1,0:T(8,128)(2,1)S(1)}, bf16[48,2048]{1,0:T(8,128)(2,1)S(1)}, u32[]{:S(2)}, u32[]{:S(2)}) %collective-permute-start.13) | collective-permute-done | bytes 196640 | tf_op jit(solution)/shard_map/ppermute | solution.py:65
  211.6 7.4 %collective-permute-done.45 = bf16[48,2048]{1,0:T(8,128)(2,1)S(1)} collective-permute-done((bf16[48,2048]{1,0:T(8,128)(2,1)S(1)}, bf16[48,2048]{1,0:T(8,128)(2,1)S(1)}, u32[]{:S(2)}, u32[]{:S(2)}) %collective-permute-start.45) | collective-permute-done | bytes 196640 | tf_op jit(solution)/shard_map/ppermute | solution.py:65
  219.1 9.3 %collective-permute-done.46 = bf16[48,2048]{1,0:T(8,128)(2,1)S(1)} collective-permute-done((bf16[48,2048]{1,0:T(8,128)(2,1)S(1)}, bf16[48,2048]{1,0:T(8,128)(2,1)S(1)}, u32[]{:S(2)}, u32[]{:S(2)}) %collective-permute-start.46) | collective-permute-done | bytes 196640 | tf_op jit(solution)/shard_map/ppermute | solution.py:65
  229.6 7.2 %collective-permute-done.47 = bf16[48,2048]{1,0:T(8,128)(2,1)S(1)} collective-permute-done((bf16[48,2048]{1,0:T(8,128)(2,1)S(1)}, bf16[48,2048]{1,0:T(8,128)(2,1)S(1)}, u32[]{:S(2)}, u32[]{:S(2)}) %collective-permute-start.47) | collective-permute-done | bytes 196640 | tf_op jit(solution)/shard_map/ppermute | solution.py:65
  239.0 6.2 collective-permute-done.48
  256.6 6.2 collective-permute-done.16
  263.2 7.7 %collective-permute-done.17 = bf16[48,2048]{1,0:T(8,128)(2,1)S(1)} collective-permute-done((bf16[48,2048]{1,0:T(8,128)(2,1)S(1)}, bf16[48,2048]{1,0:T(8,128)(2,1)S(1)}, u32[]{:S(2)}, u32[]{:S(2)}) %collective-permute-start.17) | collective-permute-done | bytes 196640 | tf_op jit(solution)/shard_map/ppermute | solution.py:65
  276.6 55.8 %collective-permute-done = bf16[48,2048]{1,0:T(8,128)(2,1)S(1)} collective-permute-done((bf16[48,2048]{1,0:T(8,128)(2,1)S(1)}, bf16[48,2048]{1,0:T(8,128)(2,1)S(1)}, u32[]{:S(2)}, u32[]{:S(2)}) %collective-permute-start) | collective-permute-done | bytes 196640 | tf_op jit(solution)/shard_map/ppermute | solution.py:65
  333.1 6.9 collective-permute-done.1
  350.0 17.4 %collective-permute-done.29 = bf16[48,2048]{1,0:T(8,128)(2,1)S(1)} collective-permute-done((bf16[48,2048]{1,0:T(8,128)(2,1)S(1)}, bf16[48,2048]{1,0:T(8,128)(2,1)S(1)}, u32[]{:S(2)}, u32[]{:S(2)}) %collective-permute-start.29) | collective-permute-done | bytes 196640 | tf_op jit(solution)/shard_map/ppermute | solution.py:65
  370.4 52.5 %collective-permute-done.31 = bf16[48,2048]{1,0:T(8,128)(2,1)S(1)} collective-permute-done((bf16[48,2048]{1,0:T(8,128)(2,1)S(1)}, bf16[48,2048]{1,0:T(8,128)(2,1)S(1)}, u32[]{:S(2)}, u32[]{:S(2)}) %collective-permute-start.31) | collective-permute-done | bytes 196640 | tf_op jit(solution)/shard_map/ppermute | solution.py:65
  422.9 8.9 %collective-permute-done.32 = bf16[48,2048]{1,0:T(8,128)(2,1)S(1)} collective-permute-done((bf16[48,2048]{1,0:T(8,128)(2,1)S(1)}, bf16[48,2048]{1,0:T(8,128)(2,1)S(1)}, u32[]{:S(2)}, u32[]{:S(2)}) %collective-permute-start.32) | collective-permute-done | bytes 196640 | tf_op jit(solution)/shard_map/ppermute | solution.py:65
  433.8 7.7 %collective-permute-done.33 = bf16[48,2048]{1,0:T(8,128)(2,1)S(1)} collective-permute-done((bf16[48,2048]{1,0:T(8,128)(2,1)S(1)}, bf16[48,2048]{1,0:T(8,128)(2,1)S(1)}, u32[]{:S(2)}, u32[]{:S(2)}) %collective-permute-start.33) | collective-permute-done | bytes 196640 | tf_op jit(solution)/shard_map/ppermute | solution.py:65
  443.9 8.2 %collective-permute-done.34 = bf16[48,2048]{1,0:T(8,128)(2,1)S(1)} collective-permute-done((bf16[48,2048]{1,0:T(8,128)(2,1)S(1)}, bf16[48,2048]{1,0:T(8,128)(2,1)S(1)}, u32[]{:S(2)}, u32[]{:S(2)}) %collective-permute-start.34) | collective-permute-done | bytes 196640 | tf_op jit(solution)/shard_map/ppermute | solution.py:65
  469.0 15.6 %collective-permute-done.64 = bf16[384,2048]{1,0:T(8,128)(2,1)S(1)} collective-permute-done((bf16[384,2048]{1,0:T(8,128)(2,1)S(1)}, bf16[384,2048]{1,0:T(8,128)(2,1)S(1)}, u32[]{:S(2)}, u32[]{:S(2)}) %collective-permute-start.64) | collective-permute-done | bytes 1572896 | tf_op jit(solution)/shard_map/ppermute | solution.py:65
  488.1 13.4 %collective-permute-done.66 = bf16[384,2048]{1,0:T(8,128)(2,1)} collective-permute-done((bf16[384,2048]{1,0:T(8,128)(2,1)S(1)}, bf16[384,2048]{1,0:T(8,128)(2,1)}, u32[]{:S(2)}, u32[]{:S(2)}) %collective-permute-start.66) | collective-permute-done | bytes 1572896 | tf_op jit(solution)/shard_map/ppermute | solution.py:65
  513.5 8.9 %collective-permute-done.38 = bf16[48,2048]{1,0:T(8,128)(2,1)S(1)} collective-permute-done((bf16[48,2048]{1,0:T(8,128)(2,1)S(1)}, bf16[48,2048]{1,0:T(8,128)(2,1)S(1)}, u32[]{:S(2)}, u32[]{:S(2)}) %collective-permute-start.38) | collective-permute-done | bytes 196640 | tf_op jit(solution)/shard_map/ppermute | solution.py:65
  522.4 10.5 %collective-permute-done.39 = bf16[48,2048]{1,0:T(8,128)(2,1)S(1)} collective-permute-done((bf16[48,2048]{1,0:T(8,128)(2,1)S(1)}, bf16[48,2048]{1,0:T(8,128)(2,1)S(1)}, u32[]{:S(2)}, u32[]{:S(2)}) %collective-permute-start.39) | collective-permute-done | bytes 196640 | tf_op jit(solution)/shard_map/ppermute | solution.py:65
  534.7 6.9 collective-permute-done.40
  544.0 6.4 collective-permute-done.41
  573.8 9.3 %collective-permute-done.52 = bf16[48,2048]{1,0:T(8,128)(2,1)S(1)} collective-permute-done((bf16[48,2048]{1,0:T(8,128)(2,1)S(1)}, bf16[48,2048]{1,0:T(8,128)(2,1)S(1)}, u32[]{:S(2)}, u32[]{:S(2)}) %collective-permute-start.52) | collective-permute-done | bytes 196640 | tf_op jit(solution)/shard_map/ppermute | solution.py:65
  583.9 9.7 %collective-permute-done.53 = bf16[48,2048]{1,0:T(8,128)(2,1)S(1)} collective-permute-done((bf16[48,2048]{1,0:T(8,128)(2,1)S(1)}, bf16[48,2048]{1,0:T(8,128)(2,1)S(1)}, u32[]{:S(2)}, u32[]{:S(2)}) %collective-permute-start.53) | collective-permute-done | bytes 196640 | tf_op jit(solution)/shard_map/ppermute | solution.py:65
  596.0 6.5 collective-permute-done.54
  620.9 17.9 %collective-permute-done.68 = bf16[1,384,2048]{2,1,0:T(8,128)(2,1)S(1)} collective-permute-done((bf16[1,384,2048]{2,1,0:T(8,128)(2,1)S(1)}, bf16[1,384,2048]{2,1,0:T(8,128)(2,1)S(1)}, u32[]{:S(2)}, u32[]{:S(2)}) %collective-permute-start.68) | collective-permute-done | bytes 1572896 | tf_op jit(solution)/shard_map/ppermute | solution.py:68
  658.4 35.5 %psum.7 = f32[192,2]{0,1:T(2,128)S(1)} all-reduce(f32[192,2]{0,1:T(2,128)S(1)} %pad_maximum_fusion.6), channel_id=1, replica_groups=mesh['dom'=8,'neu'=4] {'neu'}, use_global_device_ids=true, to_apply=%region_9.10 | all-reduce | flops 384 | bytes 3072 | tf_op jit(solution)/shard_map/psum | solution.py:188
  (432 shorter events, 278.8 us)
Async XLA Ops:
  7.9 77.3 %collective-permute-start.62 = (bf16[48,128]{1,0:T(8,128)(2,1)}, bf16[48,128]{1,0:T(8,128)(2,1)}, u32[]{:S(2)}, u32[]{:S(2)}) collective-permute-start(bf16[48,128]{1,0:T(8,128)(2,1)} %get-tuple-element.118), channel_id=1, source_target_pairs={{0,28},{4,24},{8,20},{12,16},{16,12},{20,8},{24,4},{28,0},{1,29},{... | collective-permute-start | bytes 36872 | tf_op jit(solution)/shard_map/ppermute | solution.py:65
  13.9 68.1 %collective-permute-start.61 = (bf16[48,128]{1,0:T(8,128)(2,1)}, bf16[48,128]{1,0:T(8,128)(2,1)}, u32[]{:S(2)}, u32[]{:S(2)}) collective-permute-start(bf16[48,128]{1,0:T(8,128)(2,1)} %get-tuple-element.119), channel_id=1, source_target_pairs={{0,24},{4,28},{8,16},{12,20},{16,8},{20,12},{24,0},{28,4},{1,25},{... | collective-permute-start | bytes 36872 | tf_op jit(solution)/shard_map/ppermute | solution.py:65
  14.1 65.6 %collective-permute-start.60 = (bf16[48,128]{1,0:T(8,128)(2,1)}, bf16[48,128]{1,0:T(8,128)(2,1)}, u32[]{:S(2)}, u32[]{:S(2)}) collective-permute-start(bf16[48,128]{1,0:T(8,128)(2,1)} %get-tuple-element.120), channel_id=1, source_target_pairs={{0,20},{4,16},{8,28},{12,24},{16,4},{20,0},{24,12},{28,8},{1,21},{... | collective-permute-start | bytes 36872 | tf_op jit(solution)/shard_map/ppermute | solution.py:65
  14.9 63.9 %collective-permute-start.59 = (bf16[48,128]{1,0:T(8,128)(2,1)}, bf16[48,128]{1,0:T(8,128)(2,1)}, u32[]{:S(2)}, u32[]{:S(2)}) collective-permute-start(bf16[48,128]{1,0:T(8,128)(2,1)} %get-tuple-element.121), channel_id=1, source_target_pairs={{0,16},{4,20},{8,24},{12,28},{16,0},{20,4},{24,8},{28,12},{1,17},{... | collective-permute-start | bytes 36872 | tf_op jit(solution)/shard_map/ppermute | solution.py:65
  16.9 49.9 %collective-permute-start.56 = (bf16[48,128]{1,0:T(8,128)(2,1)}, bf16[48,128]{1,0:T(8,128)(2,1)}, u32[]{:S(2)}, u32[]{:S(2)}) collective-permute-start(bf16[48,128]{1,0:T(8,128)(2,1)} %get-tuple-element.124), channel_id=1, source_target_pairs={{0,4},{4,0},{8,12},{12,8},{16,20},{20,16},{24,28},{28,24},{1,5},{5... | collective-permute-start | bytes 36872 | tf_op jit(solution)/shard_map/ppermute | solution.py:65
  75.2 50.8 %collective-permute-start.27 = (bf16[48,2048]{1,0:T(8,128)(2,1)S(1)}, bf16[48,2048]{1,0:T(8,128)(2,1)S(1)}, u32[]{:S(2)}, u32[]{:S(2)}) collective-permute-start(bf16[48,2048]{1,0:T(8,128)(2,1)S(1)} %copy-done.53), channel_id=1, source_target_pairs={{0,28},{4,24},{8,20},{12,16},{16,12},{20,8},{24,4},{28,0},{1,29},{... | collective-permute-start | bytes 589832 | tf_op jit(solution)/shard_map/ppermute | solution.py:65
  78.8 44.2 %collective-permute-start.26 = (bf16[48,2048]{1,0:T(8,128)(2,1)S(1)}, bf16[48,2048]{1,0:T(8,128)(2,1)}, u32[]{:S(2)}, u32[]{:S(2)}) collective-permute-start(bf16[48,2048]{1,0:T(8,128)(2,1)S(1)} %copy-done.54), channel_id=1, source_target_pairs={{0,24},{4,28},{8,16},{12,20},{16,8},{20,12},{24,0},{28,4},{1,25},{... | collective-permute-start | bytes 589832 | tf_op jit(solution)/shard_map/ppermute | solution.py:65
  79.7 41.7 %collective-permute-start.25 = (bf16[48,2048]{1,0:T(8,128)(2,1)S(1)}, bf16[48,2048]{1,0:T(8,128)(2,1)}, u32[]{:S(2)}, u32[]{:S(2)}) collective-permute-start(bf16[48,2048]{1,0:T(8,128)(2,1)S(1)} %copy-done.55), channel_id=1, source_target_pairs={{0,20},{4,16},{8,28},{12,24},{16,4},{20,0},{24,12},{28,8},{1,21},{... | collective-permute-start | bytes 589832 | tf_op jit(solution)/shard_map/ppermute | solution.py:65
  82.0 36.0 %collective-permute-start.24 = (bf16[48,2048]{1,0:T(8,128)(2,1)S(1)}, bf16[48,2048]{1,0:T(8,128)(2,1)}, u32[]{:S(2)}, u32[]{:S(2)}) collective-permute-start(bf16[48,2048]{1,0:T(8,128)(2,1)S(1)} %copy-done.56), channel_id=1, source_target_pairs={{0,16},{4,20},{8,24},{12,28},{16,0},{20,4},{24,8},{28,12},{1,17},{... | collective-permute-start | bytes 589832 | tf_op jit(solution)/shard_map/ppermute | solution.py:65
  102.6 12.5 %collective-permute-start.23 = (bf16[48,2048]{1,0:T(8,128)(2,1)S(1)}, bf16[48,2048]{1,0:T(8,128)(2,1)S(1)}, u32[]{:S(2)}, u32[]{:S(2)}) collective-permute-start(bf16[48,2048]{1,0:T(8,128)(2,1)S(1)} %copy-done.57), channel_id=1, source_target_pairs={{0,12},{4,8},{8,4},{12,0},{16,28},{20,24},{24,20},{28,16},{1,13},{... | collective-permute-start | bytes 589832 | tf_op jit(solution)/shard_map/ppermute | solution.py:65
  115.1 160.4 %collective-permute-start.20 = (bf16[48,2048]{1,0:T(8,128)(2,1)S(1)}, bf16[48,2048]{1,0:T(8,128)(2,1)S(1)}, u32[]{:S(2)}, u32[]{:S(2)}) collective-permute-start(bf16[48,2048]{1,0:T(8,128)(2,1)S(1)} %copy-done.36), channel_id=1, source_target_pairs={{0,28},{4,24},{8,20},{12,16},{16,12},{20,8},{24,4},{28,0},{1,29},{... | collective-permute-start | bytes 589832 | tf_op jit(solution)/shard_map/ppermute | solution.py:65
  117.9 157.4 %collective-permute-start.19 = (bf16[48,2048]{1,0:T(8,128)(2,1)S(1)}, bf16[48,2048]{1,0:T(8,128)(2,1)S(1)}, u32[]{:S(2)}, u32[]{:S(2)}) collective-permute-start(bf16[48,2048]{1,0:T(8,128)(2,1)S(1)} %copy-done.38), channel_id=1, source_target_pairs={{0,24},{4,28},{8,16},{12,20},{16,8},{20,12},{24,0},{28,4},{1,25},{... | collective-permute-start | bytes 589832 | tf_op jit(solution)/shard_map/ppermute | solution.py:65
  121.4 151.9 %collective-permute-start.18 = (bf16[48,2048]{1,0:T(8,128)(2,1)S(1)}, bf16[48,2048]{1,0:T(8,128)(2,1)S(1)}, u32[]{:S(2)}, u32[]{:S(2)}) collective-permute-start(bf16[48,2048]{1,0:T(8,128)(2,1)S(1)} %copy-done.39), channel_id=1, source_target_pairs={{0,20},{4,16},{8,28},{12,24},{16,4},{20,0},{24,12},{28,8},{1,21},{... | collective-permute-start | bytes 589832 | tf_op jit(solution)/shard_map/ppermute | solution.py:65
  123.0 126.8 %collective-permute-start.14 = (bf16[48,2048]{1,0:T(8,128)(2,1)}, bf16[48,2048]{1,0:T(8,128)(2,1)S(1)}, u32[]{:S(2)}, u32[]{:S(2)}) collective-permute-start(bf16[48,2048]{1,0:T(8,128)(2,1)} %get-tuple-element.92), channel_id=1, source_target_pairs={{0,4},{4,0},{8,12},{12,8},{16,20},{20,16},{24,28},{28,24},{1,5},{5... | collective-permute-start | bytes 589832 | tf_op jit(solution)/shard_map/ppermute | solution.py:65
  152.9 12.7 %collective-permute-start.10 = (bf16[48,2048]{1,0:T(8,128)(2,1)S(1)}, bf16[48,2048]{1,0:T(8,128)(2,1)S(1)}, u32[]{:S(2)}, u32[]{:S(2)}) collective-permute-start(bf16[48,2048]{1,0:T(8,128)(2,1)S(1)} %copy-done.50), channel_id=1, source_target_pairs={{0,16},{4,20},{8,24},{12,28},{16,0},{20,4},{24,8},{28,12},{1,17},{... | collective-permute-start | bytes 589832 | tf_op jit(solution)/shard_map/ppermute | solution.py:65
  245.3 216.1 %collective-permute-start.63 = (bf16[2048,1024]{1,0:T(8,128)(2,1)S(1)}, bf16[2048,1024]{1,0:T(8,128)(2,1)S(1)}, u32[]{:S(2)}, u32[]{:S(2)}) collective-permute-start(bf16[2048,1024]{1,0:T(8,128)(2,1)S(1)} %copy-done), channel_id=1, source_target_pairs={{0,4},{4,0},{8,12},{12,8},{16,20},{20,16},{24,28},{28,24},{1,5},{5... | collective-permute-start | bytes 12582920 | tf_op jit(solution)/shard_map/ppermute | solution.py:65
  270.9 379.9 %collective-permute-start.6 = (bf16[48,2048]{1,0:T(8,128)(2,1)S(1)}, bf16[48,2048]{1,0:T(8,128)(2,1)}, u32[]{:S(2)}, u32[]{:S(2)}) collective-permute-start(bf16[48,2048]{1,0:T(8,128)(2,1)S(1)} %get-tuple-element.102), channel_id=1, source_target_pairs={{0,28},{4,24},{8,20},{12,16},{16,12},{20,8},{24,4},{28,0},{1,29},{... | collective-permute-start | bytes 589832 | tf_op jit(solution)/shard_map/ppermute | solution.py:65
  273.3 371.4 %collective-permute-start.5 = (bf16[48,2048]{1,0:T(8,128)(2,1)S(1)}, bf16[48,2048]{1,0:T(8,128)(2,1)}, u32[]{:S(2)}, u32[]{:S(2)}) collective-permute-start(bf16[48,2048]{1,0:T(8,128)(2,1)S(1)} %get-tuple-element.103), channel_id=1, source_target_pairs={{0,24},{4,28},{8,16},{12,20},{16,8},{20,12},{24,0},{28,4},{1,25},{... | collective-permute-start | bytes 589832 | tf_op jit(solution)/shard_map/ppermute | solution.py:65
  275.4 65.9 %collective-permute-start.2 = (bf16[48,2048]{1,0:T(8,128)(2,1)S(1)}, bf16[48,2048]{1,0:T(8,128)(2,1)S(1)}, u32[]{:S(2)}, u32[]{:S(2)}) collective-permute-start(bf16[48,2048]{1,0:T(8,128)(2,1)S(1)} %copy-done.34), channel_id=1, source_target_pairs={{0,12},{4,8},{8,4},{12,0},{16,28},{20,24},{24,20},{28,16},{1,13},{... | collective-permute-start | bytes 589832 | tf_op jit(solution)/shard_map/ppermute | solution.py:65
  275.5 56.8 %collective-permute-start = (bf16[48,2048]{1,0:T(8,128)(2,1)S(1)}, bf16[48,2048]{1,0:T(8,128)(2,1)S(1)}, u32[]{:S(2)}, u32[]{:S(2)}) collective-permute-start(bf16[48,2048]{1,0:T(8,128)(2,1)S(1)} %copy-done.37), channel_id=1, source_target_pairs={{0,4},{4,0},{8,12},{12,8},{16,20},{20,16},{24,28},{28,24},{1,5},{5... | collective-permute-start | bytes 589832 | tf_op jit(solution)/shard_map/ppermute | solution.py:65
  340.0 27.5 %collective-permute-start.30 = (bf16[48,2048]{1,0:T(8,128)(2,1)S(1)}, bf16[48,2048]{1,0:T(8,128)(2,1)S(1)}, u32[]{:S(2)}, u32[]{:S(2)}) collective-permute-start(bf16[48,2048]{1,0:T(8,128)(2,1)S(1)} %copy-done.31), channel_id=1, source_target_pairs={{0,12},{4,8},{8,4},{12,0},{16,28},{20,24},{24,20},{28,16},{1,13},{... | collective-permute-start | bytes 589832 | tf_op jit(solution)/shard_map/ppermute | solution.py:65
  348.9 18.5 %collective-permute-start.29 = (bf16[48,2048]{1,0:T(8,128)(2,1)S(1)}, bf16[48,2048]{1,0:T(8,128)(2,1)S(1)}, u32[]{:S(2)}, u32[]{:S(2)}) collective-permute-start(bf16[48,2048]{1,0:T(8,128)(2,1)S(1)} %copy-done.32), channel_id=1, source_target_pairs={{0,8},{4,12},{8,0},{12,4},{16,24},{20,28},{24,16},{28,20},{1,9},{5... | collective-permute-start | bytes 589832 | tf_op jit(solution)/shard_map/ppermute | solution.py:65
  367.4 91.0 %collective-permute-start.65 = (bf16[384,2048]{1,0:T(8,128)(2,1)S(1)}, bf16[384,2048]{1,0:T(8,128)(2,1)S(1)}, u32[]{:S(2)}, u32[]{:S(2)}) collective-permute-start(bf16[384,2048]{1,0:T(8,128)(2,1)S(1)} %pad_maximum_fusion.5), channel_id=1, source_target_pairs={{0,16},{4,20},{8,24},{12,28},{16,0},{20,4},{24,8},{28,12},{1,17},{... | collective-permute-start | bytes 4718600 | tf_op jit(solution)/shard_map/ppermute | solution.py:65
  367.5 55.4 %collective-permute-start.31 = (bf16[48,2048]{1,0:T(8,128)(2,1)S(1)}, bf16[48,2048]{1,0:T(8,128)(2,1)S(1)}, u32[]{:S(2)}, u32[]{:S(2)}) collective-permute-start(bf16[48,2048]{1,0:T(8,128)(2,1)S(1)} %copy-done.30), channel_id=1, source_target_pairs={{0,16},{4,20},{8,24},{12,28},{16,0},{20,4},{24,8},{28,12},{1,17},{... | collective-permute-start | bytes 589832 | tf_op jit(solution)/shard_map/ppermute | solution.py:65
  457.7 186.0 %collective-permute-start.4 = (bf16[48,2048]{1,0:T(8,128)(2,1)S(1)}, bf16[48,2048]{1,0:T(8,128)(2,1)}, u32[]{:S(2)}, u32[]{:S(2)}) collective-permute-start(bf16[48,2048]{1,0:T(8,128)(2,1)S(1)} %copy-done.16), channel_id=1, source_target_pairs={{0,20},{4,16},{8,28},{12,24},{16,4},{20,0},{24,12},{28,8},{1,21},{... | collective-permute-start | bytes 589832 | tf_op jit(solution)/shard_map/ppermute | solution.py:65
  458.4 26.2 %collective-permute-start.64 = (bf16[384,2048]{1,0:T(8,128)(2,1)S(1)}, bf16[384,2048]{1,0:T(8,128)(2,1)S(1)}, u32[]{:S(2)}, u32[]{:S(2)}) collective-permute-start(bf16[384,2048]{1,0:T(8,128)(2,1)S(1)} %pad_maximum_fusion.5), channel_id=1, source_target_pairs={{0,8},{4,12},{8,0},{12,4},{16,24},{20,28},{24,16},{28,20},{1,9},{5... | collective-permute-start | bytes 4718600 | tf_op jit(solution)/shard_map/ppermute | solution.py:65
  461.3 40.2 %collective-permute-start.66 = (bf16[384,2048]{1,0:T(8,128)(2,1)S(1)}, bf16[384,2048]{1,0:T(8,128)(2,1)}, u32[]{:S(2)}, u32[]{:S(2)}) collective-permute-start(bf16[384,2048]{1,0:T(8,128)(2,1)S(1)} %collective-permute-done.65), channel_id=1, source_target_pairs={{0,8},{4,12},{8,0},{12,4},{16,24},{20,28},{24,16},{28,20},{1,9},{5... | collective-permute-start | bytes 4718600 | tf_op jit(solution)/shard_map/ppermute | solution.py:65
  484.6 26.0 %collective-permute-start.37 = (bf16[48,2048]{1,0:T(8,128)(2,1)}, bf16[48,2048]{1,0:T(8,128)(2,1)}, u32[]{:S(2)}, u32[]{:S(2)}) collective-permute-start(bf16[48,2048]{1,0:T(8,128)(2,1)} %get-tuple-element.66), channel_id=1, source_target_pairs={{0,12},{4,8},{8,4},{12,0},{16,28},{20,24},{24,20},{28,16},{1,13},{... | collective-permute-start | bytes 589832 | tf_op jit(solution)/shard_map/ppermute | solution.py:65
  508.9 98.8 %collective-permute-start.67 = (bf16[2,384,2048]{2,1,0:T(8,128)(2,1)S(1)}, bf16[2,384,2048]{2,1,0:T(8,128)(2,1)S(1)}, u32[]{:S(2)}, u32[]{:S(2)}) collective-permute-start(bf16[2,384,2048]{2,1,0:T(8,128)(2,1)S(1)} %dynamic-slice_convert_fusion), channel_id=1, source_target_pairs={{0,1},{1,0},{2,3},{3,2},{4,5},{5,4},{6,7},{7,6},{8,9},{9,8},{10,11... | collective-permute-start | bytes 9437192 | tf_op jit(solution)/shard_map/ppermute | solution.py:68
  602.6 40.2 %collective-permute-start.3 = (bf16[48,2048]{1,0:T(8,128)(2,1)}, bf16[48,2048]{1,0:T(8,128)(2,1)}, u32[]{:S(2)}, u32[]{:S(2)}) collective-permute-start(bf16[48,2048]{1,0:T(8,128)(2,1)} %get-tuple-element.105), channel_id=1, source_target_pairs={{0,16},{4,20},{8,24},{12,28},{16,0},{20,4},{24,8},{28,12},{1,17},{... | collective-permute-start | bytes 589832 | tf_op jit(solution)/shard_map/ppermute | solution.py:65
  616.5 22.3 %collective-permute-start.68 = (bf16[1,384,2048]{2,1,0:T(8,128)(2,1)S(1)}, bf16[1,384,2048]{2,1,0:T(8,128)(2,1)S(1)}, u32[]{:S(2)}, u32[]{:S(2)}) collective-permute-start(bf16[1,384,2048]{2,1,0:T(8,128)(2,1)S(1)} %dynamic-slice_convert_fusion.1), channel_id=1, source_target_pairs={{0,2},{1,3},{2,0},{3,1},{4,6},{5,7},{6,4},{7,5},{8,10},{9,11},{10,... | collective-permute-start | bytes 4718600 | tf_op jit(solution)/shard_map/ppermute | solution.py:68
  640.5 13.2 %collective-permute-start.69 = (bf16[384,2048]{1,0:T(8,128)(2,1)}, bf16[384,2048]{1,0:T(8,128)(2,1)S(1)}, u32[]{:S(2)}, u32[]{:S(2)}) collective-permute-start(bf16[384,2048]{1,0:T(8,128)(2,1)} %fusion.16), channel_id=1, source_target_pairs={{0,0},{1,16},{2,8},{3,24},{4,4},{5,20},{6,12},{7,28},{8,9},{9,25},... | collective-permute-start | bytes 4718600 | tf_op jit(solution)/shard_map/ppermute | solution.py:166
  (126 other events, 3638.9 us)

commit v2 on v1

v2 whole, which is shorter than its diff:
```python
import functools

import jax
import jax.numpy as jnp
from jax import lax
from jax.experimental import pallas as pl
from jax.experimental.pallas import tpu as pltpu
from jax.sharding import PartitionSpec as P

BF = jnp.bfloat16
F32 = jnp.float32
I32 = jnp.int32
TAGS = 8
LANES = 128
VMEM_BYTES = 48 << 20


def bit_reverse(value, bits):
    out = 0
    for b in range(bits):
        out |= ((value >> b) & 1) << (bits - 1 - b)
    return out


def tile_of(narrow):
    return min(512, narrow)


def dot(a, b):
    return jnp.dot(a, b, preferred_element_type=F32)


def dot_nt(a, b):
    return lax.dot_general(a, b, (((1,), (1,)), ((), ())), preferred_element_type=F32)


def spread(values, index, cap):
    out = jnp.zeros(index.shape, I32)
    for k, value in enumerate(values):
        inside = (index >= k * cap) & (index < (k + 1) * cap)
        out = jnp.where(inside, value, out)
    return out


def prefix(counts_ref, row, end, groups):
    total = jnp.int32(0)
    for e in range(groups - 1):
        total = total + jnp.where(e < end, counts_ref[row, e], 0)
    return total


def column_prefix(counts_ref, column, end, groups):
    total = jnp.int32(0)
    for d in range(groups - 1):
        total = total + jnp.where(d < end, counts_ref[d, column], 0)
    return total


def partners(swapped, groups):
    me = lax.axis_index("dom")
    return [me ^ k if swapped else k for k in range(groups)]


def send_matrix(counts_ref, swapped, groups, cap, slots):
    me = lax.axis_index("dom")
    other = partners(swapped, groups)
    places = groups * cap
    place = lax.broadcasted_iota(I32, (places, 1), 0)
    shift = [prefix(counts_ref, me, other[k], groups) - k * cap for k in range(groups)]
    slot = lax.broadcasted_iota(I32, (places, slots), 1)
    return (slot == place + spread(shift, place, cap)).astype(BF)


def settle_matrix(counts_ref, swapped, groups, cap, rows):
    me = lax.axis_index("dom")
    places = groups * cap
    place = lax.broadcasted_iota(I32, (1, places), 1)
    shift, limit = [], []
    for k, partner in enumerate(partners(swapped, groups)):
        shift.append(column_prefix(counts_ref, me, partner, groups) - k * cap)
        limit.append(counts_ref[partner, me] + k * cap)
    target = jnp.where(place < spread(limit, place, cap), place + spread(shift, place, cap), -1)
    row = lax.broadcasted_iota(I32, (rows, places), 0)
    return (row == target).astype(BF)


def pool_pack_kernel(groups, cap, counts_ref, *refs):
    sources, out_refs, mat_ref = refs[: -groups - 1], refs[-groups - 1 : -1], refs[-1]
    slots = mat_ref.shape[1]

    @pl.when(pl.program_id(0) == 0)
    def _():
        mat_ref[...] = send_matrix(counts_ref, True, groups, cap, slots)

    mat = mat_ref[...]
    for p, plane in enumerate(pool_planes(*sources)):
        packed = dot(mat, plane).reshape(groups, cap, plane.shape[1]).astype(BF)
        for k in range(groups):
            out_refs[k][p] = packed[k]


def top_pack_kernel(groups, cap, counts_ref, tags_ref, *refs):
    sources, out_ref, mat_ref = refs[:-2], refs[-2], refs[-1]
    slots = mat_ref.shape[1]

    @pl.when(pl.program_id(0) == 0)
    def _():
        mat_ref[...] = send_matrix(counts_ref, False, groups, cap, slots)
        me = lax.axis_index("dom")
        place = lax.broadcasted_iota(I32, (LANES, slots), 0)
        slot = lax.broadcasted_iota(I32, (LANES, slots), 1)
        for e in range(groups):
            hit = (slot == place + prefix(counts_ref, me, e, groups)).astype(BF)
            out_ref[e, 3 * cap :, 0:LANES] = dot_nt(tags_ref[...], hit).astype(BF)

    mat = mat_ref[...]
    for p, plane in enumerate(top_planes(*sources)):
        packed = dot(mat, plane).reshape(groups, cap, plane.shape[1])
        out_ref[:, p * cap : (p + 1) * cap] = packed.astype(BF)


def either(spec_ref, first, second):
    side = spec_ref[...].astype(F32) >= 0.0
    return jnp.where(side, first.astype(F32), second.astype(F32)).astype(BF)


def used_alpha(alpha_ref, spec_ref):
    return either(spec_ref, alpha_ref[0, :, 0, :], alpha_ref[0, :, 1, :])


def unused_alpha(alpha_ref, spec_ref):
    return either(spec_ref, alpha_ref[0, :, 1, :], alpha_ref[0, :, 0, :])


def top_planes(lower_ref, gap_ref, alpha_ref, spec_ref):
    return [lower_ref[0], gap_ref[0], used_alpha(alpha_ref, spec_ref)]


def pool_planes(lower_ref, gap_ref, alpha_ref, top_alpha_ref, spec_ref):
    return [
        lower_ref[0],
        gap_ref[0],
        alpha_ref[0, :, 0, :],
        alpha_ref[0, :, 1, :],
        unused_alpha(top_alpha_ref, spec_ref),
    ]


def slopes(low, gap, chosen, split_slope):
    high = low + gap
    active = low >= 0.0
    inactive = high <= 0.0
    ratio = high / gap
    upper_slope = jnp.where(active, 1.0, jnp.where(inactive, 0.0, ratio))
    intercept = jnp.where(active | inactive | chosen, 0.0, -ratio * low)
    upper_slope = jnp.where(chosen, split_slope, upper_slope)
    return high, active, inactive, upper_slope, intercept


def lower_slope_of(alpha, active, inactive, chosen, split_slope):
    slope = jnp.where(active, 1.0, jnp.where(inactive, 0.0, alpha))
    return jnp.where(chosen, split_slope, slope)


def row_facts(tags):
    neuron = tags[:, 0:1] * 128.0 + tags[:, 1:2]
    active_branch = tags[:, 2:3]
    split_slope = jnp.where(active_branch == 1.0, 1.0, 0.0)
    penalty = [tags[:, 3 + s : 4 + s] * (2.0 * active_branch - 1.0) for s in range(2)]
    return neuron.astype(I32), split_slope, penalty


def stacked(in_refs, plane):
    return jnp.concatenate([ref[plane] for ref in in_refs], axis=0)


def top_kernel(groups, cap, counts_ref, in_ref, spec_ref, *refs):
    lower_ref, gap_ref, used_ref, relaxed_ref, moved_ref, offset_ref, mat_ref = refs
    rows, tile = used_ref.shape
    step = pl.program_id(0)
    narrow = tile * pl.num_programs(0)

    @pl.when(step == 0)
    def _():
        mat_ref[...] = settle_matrix(counts_ref, False, groups, cap, rows)
        me = lax.axis_index("dom")
        row = lax.broadcasted_iota(I32, (rows, LANES), 0)
        place = lax.broadcasted_iota(I32, (rows, LANES), 1)
        moved = jnp.zeros((rows, TAGS), F32)
        for d in range(groups):
            first = column_prefix(counts_ref, me, d, groups)
            hit = ((row - place == first) & (place < counts_ref[d, me])).astype(BF)
            moved = moved + dot_nt(hit, in_ref[d, 3 * cap :, 0:LANES])
        moved_ref[...] = moved
        offset_ref[...] = jnp.zeros_like(offset_ref)

    mat = mat_ref[...]
    low, gap, used = (
        dot(mat, in_ref[:, p * cap : (p + 1) * cap].reshape(groups * cap, tile)) for p in range(3)
    )
    lower_ref[0] = low.astype(BF)
    gap_ref[0] = gap.astype(BF)
    used_ref[...] = used.astype(BF)
    neuron, split_slope, penalty = row_facts(moved_ref[...])
    base = (lax.axis_index("neu") + lax.axis_size("neu")) * narrow + step * tile
    chosen = neuron == base + lax.broadcasted_iota(I32, (rows, tile), 1)
    high, active, inactive, upper_slope, intercept = slopes(low, gap, chosen, split_slope)
    lower_slope = lower_slope_of(used, active, inactive, chosen, split_slope)
    spec = spec_ref[...].astype(F32)
    sums = []
    for s in range(2):
        coeff = spec if s == 0 else -spec
        negative = jnp.minimum(coeff, 0.0)
        value = jnp.maximum(coeff, 0.0) * lower_slope + negative * upper_slope
        value = value - jnp.where(chosen, penalty[s], 0.0)
        relaxed_ref[s] = value.astype(BF)
        sums.append(jnp.sum(negative * intercept, axis=1, keepdims=True))
    offset_ref[...] += jnp.concatenate(sums, axis=1)


def low_kernel(groups, cap, counts_ref, *refs):
    in_refs, refs = refs[:groups], refs[groups:]
    coeff_ref, tags_ref, before_ref, used_ref, spec_ref, _, _, *refs = refs
    lower_ref, gap_ref, alpha_ref, offset_ref, mat_ref = refs
    rows, tile = used_ref.shape
    step = pl.program_id(0)
    narrow = tile * pl.num_programs(0)

    @pl.when(step == 0)
    def _():
        mat_ref[...] = settle_matrix(counts_ref, True, groups, cap, rows)
        offset_ref[...] = before_ref[...]

    mat = mat_ref[...]
    low, gap, *alpha, rest = (dot(mat, stacked(in_refs, p)) for p in range(5))
    lower_ref[0] = low.astype(BF)
    gap_ref[0] = gap.astype(BF)
    for s in range(2):
        alpha_ref[0, :, s, :] = alpha[s].astype(BF)
    used = used_ref[...]
    alpha_ref[1, :, 0, :] = either(spec_ref, used, rest)
    alpha_ref[1, :, 1, :] = either(spec_ref, rest, used)
    neuron, split_slope, penalty = row_facts(tags_ref[...])
    base = lax.axis_index("neu") * narrow + step * tile
    chosen = neuron == base + lax.broadcasted_iota(I32, (rows, tile), 1)
    high, active, inactive, upper_slope, intercept = slopes(low, gap, chosen, split_slope)
    sums = []
    for s in range(2):
        coeff = coeff_ref[s].astype(F32)
        lower_slope = lower_slope_of(alpha[s], active, inactive, chosen, split_slope)
        negative = jnp.minimum(coeff, 0.0)
        value = jnp.maximum(coeff, 0.0) * lower_slope + negative * upper_slope
        value = value - jnp.where(chosen, penalty[s], 0.0)
        term = negative * intercept + jnp.maximum(value, 0.0) * low + jnp.minimum(value, 0.0) * high
        sums.append(jnp.sum(term, axis=1, keepdims=True))
    offset_ref[...] += jnp.concatenate(sums, axis=1)


def shards(
    state_lower,
    state_gap,
    state_alpha,
    split_beta,
    split_neuron,
    split_sign,
    send_counts,
    spec_row,
    weight,
):
    groups = lax.axis_size("dom")
    cores = lax.axis_size("neu")
    near = groups // cores
    bits = cores.bit_length() - 1
    assert near * cores == groups and 1 << bits == cores
    device_pos = lax.axis_index("dom")
    core_pos = lax.axis_index("neu")
    slots = state_lower.shape[1]
    rows = slots // 2
    cap = slots // groups
    places = groups * cap
    narrow = state_lower.shape[2]
    tile = tile_of(narrow)
    grid = (narrow // tile,)
    counts = send_counts.astype(I32)
    spec = spec_row[None, :]
    params = pltpu.CompilerParams(vmem_limit_bytes=VMEM_BYTES)

    smem = pl.BlockSpec(memory_space=pltpu.SMEM)

    def plane_spec(layer, count):
        return pl.BlockSpec((1, count, tile), lambda i: (layer, 0, i))

    def pair_spec(layer, count):
        return pl.BlockSpec((1, count, 2, tile), lambda i: (layer, 0, 0, i))

    def part_spec(planes):
        return pl.BlockSpec((planes, cap, tile), lambda i: (0, 0, i))

    def whole(*shape):
        return pl.BlockSpec(shape, lambda i: (0,) * len(shape))

    spec_spec = pl.BlockSpec((1, tile), lambda i: (0, i))
    flat_spec = pl.BlockSpec((rows, tile), lambda i: (0, i))
    both_spec = pl.BlockSpec((2, rows, tile), lambda i: (0, 0, i))

    def swap(value, mask):
        return lax.ppermute(value, "dom", [(d, d ^ mask) for d in range(groups)])

    def swap_core(value, mask):
        return lax.ppermute(value, "neu", [(c, c ^ mask) for c in range(cores)])

    def after(value, *others):
        return lax.optimization_barrier((value,) + others)[0]

    tags = jnp.concatenate(
        [
            (split_neuron >> 7).astype(BF)[None],
            (split_neuron & 127).astype(BF)[None],
            split_sign.astype(BF)[None],
            split_beta.T,
            jnp.zeros((TAGS - 5, slots), BF),
        ],
        axis=0,
    )
    top_rows = 3 * cap + TAGS
    top_spec = pl.BlockSpec((groups, top_rows, tile), lambda i: (0, 0, i))
    packed_top = pl.pallas_call(
        functools.partial(top_pack_kernel, groups, cap),
        grid=grid,
        in_specs=[
            smem,
            whole(TAGS, slots),
            plane_spec(1, slots),
            plane_spec(1, slots),
            pair_spec(1, slots),
            spec_spec,
        ],
        out_specs=top_spec,
        out_shape=jax.ShapeDtypeStruct((groups, top_rows, narrow), BF),
        scratch_shapes=[pltpu.VMEM((places, slots), BF)],
        compiler_params=params,
    )(counts, tags, state_lower, state_gap, state_alpha, spec)
    in_top = lax.all_to_all(packed_top, "dom", split_axis=0, concat_axis=0, tiled=True)

    pool = pl.pallas_call(
        functools.partial(pool_pack_kernel, groups, cap),
        grid=grid,
        in_specs=[
            smem,
            plane_spec(0, slots),
            plane_spec(0, slots),
            pair_spec(0, slots),
            pair_spec(1, slots),
            spec_spec,
        ],
        out_specs=[part_spec(5)] * groups,
        out_shape=[jax.ShapeDtypeStruct((5, cap, narrow), BF)] * groups,
        scratch_shapes=[pltpu.VMEM((places, slots), BF)],
        compiler_params=params,
    )(counts, state_lower, state_gap, state_alpha, state_alpha, spec)

    panel = after(weight, in_top, pool[0])
    near_panels = []
    step = 1
    while step < near:
        other = swap(panel, step)
        near_panels.append(other)
        low_side = (device_pos & step) == 0
        panel = jnp.concatenate(
            [jnp.where(low_side, panel, other), jnp.where(low_side, other, panel)], axis=1
        )
        step *= 2

    in_top, pool = lax.optimization_barrier((in_top, pool))
    moved_lower, moved_gap, used_top, relaxed_top, moved_tags, offset = pl.pallas_call(
        functools.partial(top_kernel, groups, cap),
        grid=grid,
        in_specs=[smem, top_spec, spec_spec],
        out_specs=[
            plane_spec(1, rows),
            plane_spec(1, rows),
            flat_spec,
            both_spec,
            whole(rows, TAGS),
            whole(rows, 2),
        ],
        out_shape=[
            jax.ShapeDtypeStruct((2, rows, narrow), BF),
            jax.ShapeDtypeStruct((2, rows, narrow), BF),
            jax.ShapeDtypeStruct((rows, narrow), BF),
            jax.ShapeDtypeStruct((2, rows, narrow), BF),
            jax.ShapeDtypeStruct((rows, TAGS), F32),
            jax.ShapeDtypeStruct((rows, 2), F32),
        ],
        scratch_shapes=[pltpu.VMEM((rows, places), BF)],
        compiler_params=params,
    )(counts, in_top, spec)

    half = groups // 2
    order = list(range(half, groups)) + list(range(near, half)) + list(range(1, near))
    cut = [0, groups // 8, 3 * groups // 8, 5 * groups // 8, groups - 1]
    arrived = {0: pool[0]}

    def send_pool(stage, ready, *others):
        parts = order[cut[stage] : cut[stage + 1]]
        for k in parts:
            arrived[k] = swap(after(pool[k], *others), k)
        return after(ready, *[arrived[k] for k in parts])

    held = {0: relaxed_top.reshape(2 * rows, narrow)}
    for b in reversed(range(bits)):
        for delta in [d for d in held if d | (1 << b) not in held]:
            held[delta | (1 << b)] = swap(held[delta], near << b)
        if b == bits - 1:
            held[1 << b] = send_pool(0, held[1 << b], in_top)
            if bits > 1:
                held[1] = swap(held[0], near)
                held[1 << b] = after(held[1 << b], held[1], *near_panels)
    held[cores - 1] = send_pool(1, held[cores - 1], held[cores // 2])
    partial = jnp.stack([dot(held[d], panel).astype(BF) for d in range(cores)])

    for b in range(bits):
        side = (core_pos >> b) & 1
        half = partial.shape[0] // 2
        keep = lax.dynamic_slice_in_dim(partial, side * half, half, 0)
        give = lax.dynamic_slice_in_dim(partial, (1 - side) * half, half, 0)
        taken = swap_core(give, 1 << b)
        if b == bits - 1:
            taken = send_pool(2, taken, give)
        partial = (keep.astype(F32) + taken.astype(F32)).astype(BF)
    route = []
    for o in range(cores):
        for x in range(near):
            for c in range(cores):
                to = o ^ bit_reverse(c, bits)
                route.append(((o * near + x) * cores + c, (to * near + x) * cores + o))
    coeff_low = lax.ppermute(partial[0], ("dom", "neu"), route)

    coeff_low = send_pool(3, coeff_low, partial)

    hbm = pl.BlockSpec(memory_space=pl.ANY)
    moved_lower, moved_gap, moved_alpha, offset = pl.pallas_call(
        functools.partial(low_kernel, groups, cap),
        grid=grid,
        in_specs=[smem]
        + [part_spec(5)] * groups
        + [both_spec, whole(rows, TAGS), whole(rows, 2), flat_spec, spec_spec, hbm, hbm],
        out_specs=[
            plane_spec(0, rows),
            plane_spec(0, rows),
            pl.BlockSpec((2, rows, 2, tile), lambda i: (0, 0, 0, i)),
            whole(rows, 2),
        ],
        out_shape=[
            jax.ShapeDtypeStruct((2, rows, narrow), BF),
            jax.ShapeDtypeStruct((2, rows, narrow), BF),
            jax.ShapeDtypeStruct((2, rows, 2, narrow), BF),
            jax.ShapeDtypeStruct((rows, 2), F32),
        ],
        input_output_aliases={groups + 6: 0, groups + 7: 1},
        scratch_shapes=[pltpu.VMEM((rows, places), BF)],
        compiler_params=params,
    )(
        counts,
        *[arrived[k] for k in range(groups)],
        coeff_low.reshape(2, rows, narrow),
        moved_tags,
        offset,
        used_top,
        spec,
        moved_lower,
        moved_gap,
    )

    totals = lax.psum(offset, "neu")
    bounds = jnp.stack([totals[:, 0], -totals[:, 1]], axis=1)
    neuron_ids = moved_tags[:, 0].astype(I32) * 128 + moved_tags[:, 1].astype(I32)
    sign_ids = moved_tags[:, 2].astype(I32)
    moved_beta = moved_tags[:, 3:5].astype(BF)
    return (moved_lower, moved_gap, moved_alpha, moved_beta, neuron_ids, sign_ids, bounds)


def solution(mesh):
    in_specs = (
        P(None, "dom", "neu"),
        P(None, "dom", "neu"),
        P(None, "dom", None, "neu"),
        P("dom", None),
        P("dom"),
        P("dom"),
        P(),
        P("neu"),
        P("neu", "dom"),
    )
    out_specs = (
        P(None, "dom", "neu"),
        P(None, "dom", "neu"),
        P(None, "dom", None, "neu"),
        P("dom", None),
        P("dom"),
        P("dom"),
        P("dom", None),
    )
    return jax.shard_map(shards, mesh=mesh, in_specs=in_specs, out_specs=out_specs, check_vma=False)
```

time: 702 us -> 490 us (0.70)
  waiting for transfers between devices: 438 us -> 334 us
  local copies, waits for them, and re-layouts: 64.6 us -> 14 us
  starting transfers between devices: 89.7 us -> 44.2 us
  Pallas kernels: 0 us -> 38.7 us
  matrix products: 48.7 us -> 19.5 us
  blocking collectives: 35.5 us -> 21.7 us
    ppermute x67 -> x11, waiting for transfers between devices: 421 us -> 232 us  [swap(): return lax.ppermute(value, 'dom', [(d, d ^ mask) for d in range(groups)])]
    all_to_all x0 -> x1, waiting for transfers between devices: none -> 95.8 us  [shards(): lax.all_to_all(packed_top, 'dom', split_axis=0, concat_axis=0, tiled=True)]
    ppermute x67 -> x11, starting transfers between devices: 85.3 us -> 22 us  [swap(): return lax.ppermute(value, 'dom', [(d, d ^ mask) for d in range(groups)])]
    pallas_call x0 -> x4, Pallas kernels: none -> 38.7 us  [the longest x1 14.4 us: shards(): pl.pallas_call(functools.partial(pool_pack_kernel, groups, cap), grid=gri...]
    dot_general x22 -> x4, matrix products: 48.7 us -> 19.5 us  [dot(): return jnp.dot(a, b, preferred_element_type=F32)]
    unnamed x233 -> x19, local copies, waits for them, and re-layouts: 37 us -> 8.91 us
    slice x12 -> x2, local copies, waits for them, and re-layouts: 21.3 us -> 0.17 us  [the longest x1 0.09 us: shards(): bounds = jnp.stack([totals[:, 0], -totals[:, 1]], axis=1)]
    psum x1, blocking collectives: 35.5 us -> 21.7 us  [shards(): totals = lax.psum(offset, 'neu')]
  transfers between devices with their start and end apart: 70 -> 15, of which waited for: 45 -> 8; matrix products, arithmetic and copies ran while one was open for 16% -> 4% of each run, Pallas kernels for 0% -> 4%
where the time goes in v2:
time: 490 us; the launch traced here: 488 us
  waiting for transfers between devices  334 us (68%)
  starting transfers between devices  44.2 us (9%)
  Pallas kernels  38.7 us (8%)
  blocking collectives  21.7 us (4%)
  matrix products  19.5 us (4%)
  other arithmetic  15.5 us (3%)
  local copies, waits for them, and re-layouts  14 us (3%)
    ppermute x11, waiting for transfers between devices, swap(): return lax.ppermute(value, 'dom', [(d, d ^ mask) for d in range(groups)])  232 us
    all_to_all x1, waiting for transfers between devices, shards(): lax.all_to_all(packed_top, 'dom', split_axis=0, concat_axis=0, tiled=True)  95.8 us
    ppermute x11, starting transfers between devices, swap(): return lax.ppermute(value, 'dom', [(d, d ^ mask) for d in range(groups)])  22 us
    psum x1, blocking collectives, shards(): totals = lax.psum(offset, 'neu')  21.7 us
    dot_general x4, matrix products, dot(): return jnp.dot(a, b, preferred_element_type=F32)  19.5 us
    pallas_call x1, Pallas kernels, shards(): pl.pallas_call(functools.partial(pool_pack_kernel, groups, cap), grid=gri...  14.4 us
    ppermute x1, starting transfers between devices, shards(): coeff_low = lax.ppermute(partial[0], ('dom', 'neu'), route)  13.3 us
    pallas_call x1, Pallas kernels, shards(): pl.pallas_call(functools.partial(low_kernel, groups, cap), grid=grid, in_...  9.87 us
  transfers between devices with their start and end apart: 15, of which 8 were waited for; matrix products, arithmetic and copies ran while one was open for 4% of the time, Pallas kernels for 4%

profile of v2, /device:TPU:0, one launch (start us, length us, event | category | flops | bytes accessed | tf_op | source)
XLA Modules:
  0.0 487.9 jit_solution(7982078336979433876)
XLA Ops:
  3.4 1.9 copy-done
  6.0 8.1 %shard_map.144 = bf16[8,152,2048]{2,1,0:T(8,128)(2,1)} custom-call(s32[8,8]{1,0:T(8,128)S(1)} %copy-done.3, bf16[8,384]{1,0:T(8,128)(2,1)S(1)} %concatenate.6.tags_ref, bf16[2,384,2048]{2,1,0:T(8,128)(2,1)S(1)} %copy-done, bf16[2,384,2048]{2,1,0:T(8,128)(2,1)} %refs_1_.3, bf16[2,384,2,2048]{3,2,1,0:T(2,128)(2,1)} %refs_3_.1, ...), custom_call_target="tpu_custom_call" | custom-call | tf_op jit(solution)/shard_map/pallas_call | solution.py:327
  14.1 7.4 %all-to-all-start = ((bf16[8,152,2048]{2,1,0:T(8,128)(2,1)}), bf16[8,152,2048]{2,1,0:T(8,128)(2,1)}, u32[]{:S(2)}, u32[]{:S(2)}) async-start(bf16[8,152,2048]{2,1,0:T(8,128)(2,1)} %shard_map.144), calls=%async_computation | async-start | bytes 9961472 | tf_op jit(solution)/shard_map/all_to_all | solution.py:343
  21.5 14.4 %shard_map.145 = (bf16[5,48,2048]{2,1,0:T(8,128)(2,1)S(1)}, bf16[5,48,2048]{2,1,0:T(8,128)(2,1)}, bf16[5,48,2048]{2,1,0:T(8,128)(2,1)}, bf16[5,48,2048]{2,1,0:T(...) custom-call(s32[8,8]{1,0:T(8,128)S(1)} %copy-done.4, ...), custom_call_target="tpu_custom_call" | custom-call | tf_op jit(solution)/shard_map/pallas_call | solution.py:345
  35.9 95.8 %all-to-all-done.in_ref = bf16[8,152,2048]{2,1,0:T(8,128)(2,1)} async-done(((bf16[8,152,2048]{2,1,0:T(8,128)(2,1)}), bf16[8,152,2048]{2,1,0:T(8,128)(2,1)}, u32[]{:S(2)}, u32[]{:S(2)}) %all-to-all-start) | async-done | bytes 4980768 | tf_op jit(solution)/shard_map/all_to_all | solution.py:343
  131.6 1.5 collective-permute-start
  133.1 6.4 %shard_map.146 = (bf16[2,192,2048]{2,1,0:T(8,128)(2,1)}, bf16[2,192,2048]{2,1,0:T(8,128)(2,1)}, bf16[192,2048]{1,0:T(8,128)(2,1)S(1)}, bf16[2,192,2048]{2,1,0:T(...) custom-call(s32[8,8]{1,0:T(8,128)S(1)} %copy-done.4, bf16[8,152,2048]{2,1,0:T(8,128)(2,1)} %all-to-all-done.in_ref, ...), custom_call_target="tpu_custom_call" | custom-call | tf_op jit(solution)/shard_map/pallas_call | solution.py:375
  140.4 2.0 collective-permute-start.1
  143.3 108.9 %collective-permute-done.3.refs_4_ = bf16[5,48,2048]{2,1,0:T(8,128)(2,1)S(1)} collective-permute-done((bf16[5,48,2048]{2,1,0:T(8,128)(2,1)}, bf16[5,48,2048]{2,1,0:T(8,128)(2,1)S(1)}, u32[]{:S(2)}, u32[]{:S(2)}) %collective-permute-start.3) | collective-permute-done | bytes 983072 | tf_op jit(solution)/shard_map/ppermute | solution.py:307
  252.3 1.7 collective-permute-start.5
  254.0 2.6 collective-permute-start.6
  256.6 3.8 broadcast_select_fusion.1
  260.4 5.2 %fusion.2 = bf16[1,384,2048]{2,1,0:T(8,128)(2,1)S(1)} fusion(bf16[384,2048]{1,0:T(8,128)(2,1)} %collective-permute-done.2, bf16[2048,1024]{1,0:T(8,128)(2,1)S(1)} %get-tuple-element.118, bf16[2048,1024]{1,0:T(8,128)(2,1)S(1)} %get-tuple-element.117), kind=kOutput, calls=%fused_computation.12 | convolution fusion | flops 3238789120 | bytes 11534336 | tf_op jit(solution)/shard_map/dot_general | solution.py:30
  265.6 5.2 %fusion = bf16[1,384,2048]{2,1,0:T(8,128)(2,1)S(1)} fusion(bf16[384,2048]{1,0:T(8,128)(2,1)} %bitcast.1, bf16[2048,1024]{1,0:T(8,128)(2,1)S(1)} %get-tuple-element.118, bf16[2048,1024]{1,0:T(8,128)(2,1)S(1)} %get-tuple-element.117), kind=kOutput, calls=%fused_computation.10 | convolution fusion | flops 3238789120 | bytes 11534336 | tf_op jit(solution)/shard_map/dot_general | solution.py:30
  270.9 5.2 %fusion.1 = bf16[1,384,2048]{2,1,0:T(8,128)(2,1)S(1)} fusion(bf16[384,2048]{1,0:T(8,128)(2,1)} %collective-permute-done.1, bf16[2048,1024]{1,0:T(8,128)(2,1)S(1)} %get-tuple-element.118, bf16[2048,1024]{1,0:T(8,128)(2,1)S(1)} %get-tuple-element.117), kind=kOutput, calls=%fused_computation.11 | convolution fusion | flops 3238789120 | bytes 11534336 | tf_op jit(solution)/shard_map/dot_general | solution.py:30
  276.1 32.3 %collective-permute-done.5.refs_5_ = bf16[5,48,2048]{2,1,0:T(8,128)(2,1)S(1)} collective-permute-done((bf16[5,48,2048]{2,1,0:T(8,128)(2,1)S(1)}, bf16[5,48,2048]{2,1,0:T(8,128)(2,1)S(1)}, u32[]{:S(2)}, u32[]{:S(2)}) %collective-permute-start.5) | collective-permute-done | bytes 983072 | tf_op jit(solution)/shard_map/ppermute | solution.py:307
  308.4 22.3 %collective-permute-done.6.refs_6_ = bf16[5,48,2048]{2,1,0:T(8,128)(2,1)S(1)} collective-permute-done((bf16[5,48,2048]{2,1,0:T(8,128)(2,1)}, bf16[5,48,2048]{2,1,0:T(8,128)(2,1)S(1)}, u32[]{:S(2)}, u32[]{:S(2)}) %collective-permute-start.6) | collective-permute-done | bytes 983072 | tf_op jit(solution)/shard_map/ppermute | solution.py:307
  331.7 3.8 fusion.3
  336.6 2.6 copy-done.5
  339.2 2.1 constant_dynamic-slice_fusion.1
  341.3 6.0 %collective-permute-done.7 = bf16[2,384,2048]{2,1,0:T(8,128)(2,1)} collective-permute-done((bf16[2,384,2048]{2,1,0:T(8,128)(2,1)}, bf16[2,384,2048]{2,1,0:T(8,128)(2,1)}, u32[]{:S(2)}, u32[]{:S(2)}) %collective-permute-start.7) | collective-permute-done | bytes 3145760 | tf_op jit(solution)/shard_map/ppermute | solution.py:310
  347.3 4.2 add_convert_fusion
  352.8 1.5 collective-permute-start.8
  355.8 10.0 %collective-permute-start.10 = (bf16[5,48,2048]{2,1,0:T(8,128)(2,1)}, bf16[5,48,2048]{2,1,0:T(8,128)(2,1)S(1)}, u32[]{:S(2)}, u32[]{:S(2)}) collective-permute-start(bf16[5,48,2048]{2,1,0:T(8,128)(2,1)} %get-tuple-element.72), channel_id=1, source_target_pairs={{0,8},{4,12},{8,0},{12,4},{16,24},{20,28},{24,16},{28,20},{1,9},{5... | collective-permute-start | bytes 2949128 | tf_op jit(solution)/shard_map/ppermute | solution.py:307
  365.8 16.3 %collective-permute-done.9.refs_7_ = bf16[5,48,2048]{2,1,0:T(8,128)(2,1)} collective-permute-done((bf16[5,48,2048]{2,1,0:T(8,128)(2,1)}, bf16[5,48,2048]{2,1,0:T(8,128)(2,1)}, u32[]{:S(2)}, u32[]{:S(2)}) %collective-permute-start.9) | collective-permute-done | bytes 983072 | tf_op jit(solution)/shard_map/ppermute | solution.py:307
  382.1 18.6 %collective-permute-done.10.refs_2_ = bf16[5,48,2048]{2,1,0:T(8,128)(2,1)S(1)} collective-permute-done((bf16[5,48,2048]{2,1,0:T(8,128)(2,1)}, bf16[5,48,2048]{2,1,0:T(8,128)(2,1)S(1)}, u32[]{:S(2)}, u32[]{:S(2)}) %collective-permute-start.10) | collective-permute-done | bytes 983072 | tf_op jit(solution)/shard_map/ppermute | solution.py:307
  400.7 3.7 add_convert_fusion.1
  404.4 13.3 %collective-permute-start.13 = (bf16[384,2048]{1,0:T(8,128)(2,1)}, bf16[384,2048]{1,0:T(8,128)(2,1)}, u32[]{:S(2)}, u32[]{:S(2)}) collective-permute-start(bf16[384,2048]{1,0:T(8,128)(2,1)} %bitcast.6), channel_id=1, source_target_pairs={{0,0},{1,16},{2,8},{3,24},{4,4},{5,20},{6,12},{7,28},{8,9},{9,25},... | collective-permute-start | bytes 4718600 | tf_op jit(solution)/shard_map/ppermute | solution.py:437
  417.7 1.7 collective-permute-start.11
  421.0 33.3 %collective-permute-done.11.refs_1_ = bf16[5,48,2048]{2,1,0:T(8,128)(2,1)} collective-permute-done((bf16[5,48,2048]{2,1,0:T(8,128)(2,1)}, bf16[5,48,2048]{2,1,0:T(8,128)(2,1)}, u32[]{:S(2)}, u32[]{:S(2)}) %collective-permute-start.11) | collective-permute-done | bytes 983072 | tf_op jit(solution)/shard_map/ppermute | solution.py:307
  455.5 9.9 %shard_map.147 = (bf16[2,192,2048]{2,1,0:T(8,128)(2,1)}, bf16[2,192,2048]{2,1,0:T(8,128)(2,1)}, bf16[2,192,2,2048]{3,2,1,0:T(2,128)(2,1)}, f32[192,2]{1,0:T(8,128)S(1)}) custom-call(s32[8,8]{1,0:T(8,128)S(1)} %copy-done.4, bf16[5,48,2048]{2,1,0:T(8,128)(2,1)S(1)} %get-tuple-element.55.refs_0_, ...), custom_call_target="tpu_custom_call", output_to_operand_aliasing={{0}: (14, {}), {1}: (15, {})} | custom-call | tf_op jit(solution)/shard_map/pallas_call | solution.py:442
  465.3 21.7 %psum.7 = f32[192,2]{1,0:T(8,128)S(1)} all-reduce(f32[192,2]{1,0:T(8,128)S(1)} %get-tuple-element.86), channel_id=1, replica_groups=mesh['dom'=8,'neu'=4] {'neu'}, use_global_device_ids=true, to_apply=%region_0.1 | all-reduce | flops 384 | bytes 3072 | tf_op jit(solution)/shard_map/psum | solution.py:475
  (46 shorter events, 13.7 us)
Async XLA Ops:
  3.4 1.9 copy-start
  5.3 0.7 copy-start.3
  14.1 7.4 %copy-start.4 = (s32[8,8]{1,0:T(8,128)S(1)}, s32[8,8]{1,0:T(8,128)}, u32[]{:S(2)}) copy-start(s32[8,8]{1,0:T(8,128)} %counts_ref.7) | copy-start | bytes 772
  14.1 117.5 %all-to-all-start = ((bf16[8,152,2048]{2,1,0:T(8,128)(2,1)}), bf16[8,152,2048]{2,1,0:T(8,128)(2,1)}, u32[]{:S(2)}, u32[]{:S(2)}) async-start(bf16[8,152,2048]{2,1,0:T(8,128)(2,1)} %shard_map.144), calls=%async_computation | async-start | bytes 9961472 | tf_op jit(solution)/shard_map/all_to_all | solution.py:343
  131.6 120.6 %collective-permute-start = (bf16[2048,1024]{1,0:T(8,128)(2,1)}, bf16[2048,1024]{1,0:T(8,128)(2,1)}, u32[]{:S(2)}, u32[]{:S(2)}) collective-permute-start(bf16[2048,1024]{1,0:T(8,128)(2,1)} %param.17), channel_id=1, source_target_pairs={{0,4},{4,0},{8,12},{12,8},{16,20},{20,16},{24,28},{28,24},{1,5},{5... | collective-permute-start | bytes 12582920 | tf_op jit(solution)/shard_map/ppermute | solution.py:307
  139.5 0.9 copy-start.1
  140.4 111.9 %collective-permute-start.2 = (bf16[384,2048]{1,0:T(8,128)(2,1)}, bf16[384,2048]{1,0:T(8,128)(2,1)}, u32[]{:S(2)}, u32[]{:S(2)}) collective-permute-start(bf16[384,2048]{1,0:T(8,128)(2,1)} %bitcast.1), channel_id=1, source_target_pairs={{0,16},{4,20},{8,24},{12,28},{16,0},{20,4},{24,8},{28,12},{1,17},{... | collective-permute-start | bytes 4718600 | tf_op jit(solution)/shard_map/ppermute | solution.py:307
  140.4 111.9 %collective-permute-start.1 = (bf16[384,2048]{1,0:T(8,128)(2,1)}, bf16[384,2048]{1,0:T(8,128)(2,1)}, u32[]{:S(2)}, u32[]{:S(2)}) collective-permute-start(bf16[384,2048]{1,0:T(8,128)(2,1)} %bitcast.1), channel_id=1, source_target_pairs={{0,8},{4,12},{8,0},{12,4},{16,24},{20,28},{24,16},{28,20},{1,9},{5... | collective-permute-start | bytes 4718600 | tf_op jit(solution)/shard_map/ppermute | solution.py:307
  142.4 109.8 %collective-permute-start.3 = (bf16[5,48,2048]{2,1,0:T(8,128)(2,1)}, bf16[5,48,2048]{2,1,0:T(8,128)(2,1)S(1)}, u32[]{:S(2)}, u32[]{:S(2)}) collective-permute-start(bf16[5,48,2048]{2,1,0:T(8,128)(2,1)} %get-tuple-element.61), channel_id=1, source_target_pairs={{0,16},{4,20},{8,24},{12,28},{16,0},{20,4},{24,8},{28,12},{1,17},{... | collective-permute-start | bytes 2949128 | tf_op jit(solution)/shard_map/ppermute | solution.py:307
  252.3 79.5 %collective-permute-start.4 = (bf16[384,2048]{1,0:T(8,128)(2,1)}, bf16[384,2048]{1,0:T(8,128)(2,1)S(1)}, u32[]{:S(2)}, u32[]{:S(2)}) collective-permute-start(bf16[384,2048]{1,0:T(8,128)(2,1)} %collective-permute-done.2), channel_id=1, source_target_pairs={{0,8},{4,12},{8,0},{12,4},{16,24},{20,28},{24,16},{28,20},{1,9},{5... | collective-permute-start | bytes 4718600 | tf_op jit(solution)/shard_map/ppermute | solution.py:307
  252.3 56.1 %collective-permute-start.5 = (bf16[5,48,2048]{2,1,0:T(8,128)(2,1)S(1)}, bf16[5,48,2048]{2,1,0:T(8,128)(2,1)S(1)}, u32[]{:S(2)}, u32[]{:S(2)}) collective-permute-start(bf16[5,48,2048]{2,1,0:T(8,128)(2,1)S(1)} %get-tuple-element.65), channel_id=1, source_target_pairs={{0,20},{4,16},{8,28},{12,24},{16,4},{20,0},{24,12},{28,8},{1,21},{... | collective-permute-start | bytes 2949128 | tf_op jit(solution)/shard_map/ppermute | solution.py:307
  254.0 76.7 %collective-permute-start.6 = (bf16[5,48,2048]{2,1,0:T(8,128)(2,1)}, bf16[5,48,2048]{2,1,0:T(8,128)(2,1)S(1)}, u32[]{:S(2)}, u32[]{:S(2)}) collective-permute-start(bf16[5,48,2048]{2,1,0:T(8,128)(2,1)} %get-tuple-element.67), channel_id=1, source_target_pairs={{0,24},{4,28},{8,16},{12,20},{16,8},{20,12},{24,0},{28,4},{1,25},{... | collective-permute-start | bytes 2949128 | tf_op jit(solution)/shard_map/ppermute | solution.py:307
  308.4 22.4 %copy-start.7 = (bf16[5,48,2048]{2,1,0:T(8,128)(2,1)}, bf16[5,48,2048]{2,1,0:T(8,128)(2,1)S(1)}, u32[]{:S(2)}) copy-start(bf16[5,48,2048]{2,1,0:T(8,128)(2,1)S(1)} %collective-permute-done.5.refs_5_) | copy-start | bytes 2949124
  330.7 1.0 copy-start.8
  336.5 2.7 copy-start.5
  341.3 6.0 %collective-permute-start.7 = (bf16[2,384,2048]{2,1,0:T(8,128)(2,1)}, bf16[2,384,2048]{2,1,0:T(8,128)(2,1)}, u32[]{:S(2)}, u32[]{:S(2)}) collective-permute-start(bf16[2,384,2048]{2,1,0:T(8,128)(2,1)} %constant_dynamic-slice_fusion.1), channel_id=1, source_target_pairs={{0,1},{1,0},{2,3},{3,2},{4,5},{5,4},{6,7},{7,6},{8,9},{9,8},{10,11... | collective-permute-start | bytes 9437192 | tf_op jit(solution)/shard_map/ppermute | solution.py:310
  351.5 2.9 copy-start.6
  352.8 47.9 %collective-permute-start.8 = (bf16[1,384,2048]{2,1,0:T(8,128)(2,1)}, bf16[1,384,2048]{2,1,0:T(8,128)(2,1)}, u32[]{:S(2)}, u32[]{:S(2)}) collective-permute-start(bf16[1,384,2048]{2,1,0:T(8,128)(2,1)} %constant_dynamic-slice_fusion), channel_id=1, source_target_pairs={{0,2},{1,3},{2,0},{3,1},{4,6},{5,7},{6,4},{7,5},{8,10},{9,11},{10,... | collective-permute-start | bytes 4718600 | tf_op jit(solution)/shard_map/ppermute | solution.py:310
  354.4 27.7 %collective-permute-start.9 = (bf16[5,48,2048]{2,1,0:T(8,128)(2,1)}, bf16[5,48,2048]{2,1,0:T(8,128)(2,1)}, u32[]{:S(2)}, u32[]{:S(2)}) collective-permute-start(bf16[5,48,2048]{2,1,0:T(8,128)(2,1)} %get-tuple-element.70), channel_id=1, source_target_pairs={{0,28},{4,24},{8,20},{12,16},{16,12},{20,8},{24,4},{28,0},{1,29},{... | collective-permute-start | bytes 2949128 | tf_op jit(solution)/shard_map/ppermute | solution.py:307
  355.8 44.9 %collective-permute-start.10 = (bf16[5,48,2048]{2,1,0:T(8,128)(2,1)}, bf16[5,48,2048]{2,1,0:T(8,128)(2,1)S(1)}, u32[]{:S(2)}, u32[]{:S(2)}) collective-permute-start(bf16[5,48,2048]{2,1,0:T(8,128)(2,1)} %get-tuple-element.72), channel_id=1, source_target_pairs={{0,8},{4,12},{8,0},{12,4},{16,24},{20,28},{24,16},{28,20},{1,9},{5... | collective-permute-start | bytes 2949128 | tf_op jit(solution)/shard_map/ppermute | solution.py:307
  404.4 49.9 %collective-permute-start.13 = (bf16[384,2048]{1,0:T(8,128)(2,1)}, bf16[384,2048]{1,0:T(8,128)(2,1)}, u32[]{:S(2)}, u32[]{:S(2)}) collective-permute-start(bf16[384,2048]{1,0:T(8,128)(2,1)} %bitcast.6), channel_id=1, source_target_pairs={{0,0},{1,16},{2,8},{3,24},{4,4},{5,20},{6,12},{7,28},{8,9},{9,25},... | collective-permute-start | bytes 4718600 | tf_op jit(solution)/shard_map/ppermute | solution.py:437
  417.7 36.7 %collective-permute-start.11 = (bf16[5,48,2048]{2,1,0:T(8,128)(2,1)}, bf16[5,48,2048]{2,1,0:T(8,128)(2,1)}, u32[]{:S(2)}, u32[]{:S(2)}) collective-permute-start(bf16[5,48,2048]{2,1,0:T(8,128)(2,1)} %get-tuple-element.74), channel_id=1, source_target_pairs={{0,4},{4,0},{8,12},{12,8},{16,20},{20,16},{24,28},{28,24},{1,5},{5... | collective-permute-start | bytes 2949128 | tf_op jit(solution)/shard_map/ppermute | solution.py:307
  419.4 34.9 %collective-permute-start.12 = (bf16[5,48,2048]{2,1,0:T(8,128)(2,1)}, bf16[5,48,2048]{2,1,0:T(8,128)(2,1)}, u32[]{:S(2)}, u32[]{:S(2)}) collective-permute-start(bf16[5,48,2048]{2,1,0:T(8,128)(2,1)} %get-tuple-element.76), channel_id=1, source_target_pairs={{0,12},{4,8},{8,4},{12,0},{16,28},{20,24},{24,20},{28,16},{1,13},{... | collective-permute-start | bytes 2949128 | tf_op jit(solution)/shard_map/ppermute | solution.py:307
  454.3 1.1 copy-start.2

commit v3 on v2

--- a/solution.py
+++ b/solution.py
@@ -12,6 +12,8 @@
 I32 = jnp.int32
 TAGS = 8
 LANES = 128
+LOW_PLANES = 4
+PLANES = 5
 VMEM_BYTES = 48 << 20
 
 
@@ -218,36 +220,59 @@
     offset_ref[...] += jnp.concatenate(sums, axis=1)
 
 
-def low_kernel(groups, cap, counts_ref, *refs):
+def settle_kernel(groups, cap, counts_ref, *refs):
     in_refs, refs = refs[:groups], refs[groups:]
-    coeff_ref, tags_ref, before_ref, used_ref, spec_ref, _, _, *refs = refs
-    lower_ref, gap_ref, alpha_ref, offset_ref, mat_ref = refs
-    rows, tile = used_ref.shape
+    _, _, lower_ref, gap_ref, alpha_ref, mat_ref = refs
+    rows = mat_ref.shape[0]
+
+    @pl.when(pl.program_id(0) == 0)
+    def _():
+        mat_ref[...] = settle_matrix(counts_ref, True, groups, cap, rows)
+
+    mat = mat_ref[...]
+    low, gap, *alpha = (
+        dot(mat, stacked(in_refs, p)).astype(BF) for p in range(LOW_PLANES)
+    )
+    lower_ref[0] = low
+    gap_ref[0] = gap
+    for s in range(2):
+        alpha_ref[0, :, s, :] = alpha[s]
+
+
+def rest_kernel(groups, cap, counts_ref, *refs):
+    in_refs, (used_ref, spec_ref, _, alpha_ref, mat_ref) = refs[:groups], refs[groups:]
+    rows = mat_ref.shape[0]
+
+    @pl.when(pl.program_id(0) == 0)
+    def _():
+        mat_ref[...] = settle_matrix(counts_ref, True, groups, cap, rows)
+
+    rest = dot(mat_ref[...], stacked(in_refs, 0)).astype(BF)
+    used = used_ref[...]
+    alpha_ref[0, :, 0, :] = either(spec_ref, used, rest)
+    alpha_ref[0, :, 1, :] = either(spec_ref, rest, used)
+
+
+def low_kernel(coeff_ref, tags_ref, before_ref, lower_ref, gap_ref, alpha_ref, offset_ref):
+    rows, tile = lower_ref.shape[1:]
     step = pl.program_id(0)
     narrow = tile * pl.num_programs(0)
 
     @pl.when(step == 0)
     def _():
-        mat_ref[...] = settle_matrix(counts_ref, True, groups, cap, rows)
         offset_ref[...] = before_ref[...]
 
-    mat = mat_ref[...]
-    low, gap, *alpha, rest = (dot(mat, stacked(in_refs, p)) for p in range(5))
-    lower_ref[0] = low.astype(BF)
-    gap_ref[0] = gap.astype(BF)
-    for s in range(2):
-        alpha_ref[0, :, s, :] = alpha[s].astype(BF)
-    used = used_ref[...]
-    alpha_ref[1, :, 0, :] = either(spec_ref, used, rest)
-    alpha_ref[1, :, 1, :] = either(spec_ref, rest, used)
+    low = lower_ref[0].astype(F32)
+    gap = gap_ref[0].astype(F32)
     neuron, split_slope, penalty = row_facts(tags_ref[...])
     base = lax.axis_index("neu") * narrow + step * tile
     chosen = neuron == base + lax.broadcasted_iota(I32, (rows, tile), 1)
     high, active, inactive, upper_slope, intercept = slopes(low, gap, chosen, split_slope)
     sums = []
     for s in range(2):
+        alpha = alpha_ref[0, :, s, :].astype(F32)
         coeff = coeff_ref[s].astype(F32)
-        lower_slope = lower_slope_of(alpha[s], active, inactive, chosen, split_slope)
+        lower_slope = lower_slope_of(alpha, active, inactive, chosen, split_slope)
         negative = jnp.minimum(coeff, 0.0)
         value = jnp.maximum(coeff, 0.0) * lower_slope + negative * upper_slope
         value = value - jnp.where(chosen, penalty[s], 0.0)
@@ -342,6 +367,14 @@
     )(counts, tags, state_lower, state_gap, state_alpha, spec)
     in_top = lax.all_to_all(packed_top, "dom", split_axis=0, concat_axis=0, tiled=True)
 
+    half, quarter = groups // 2, groups // 8
+    far = [list(range(half + i * quarter, half + (i + 1) * quarter)) for i in range(4)]
+    mid = list(range(near, half))
+    stages = [
+        far[0] + mid[: len(mid) // 2],
+        far[1] + far[3] + list(range(1, near)),
+        far[2] + mid[len(mid) // 2 :],
+    ]
     pool = pl.pallas_call(
         functools.partial(pool_pack_kernel, groups, cap),
         grid=grid,
@@ -353,8 +386,8 @@
             pair_spec(1, slots),
             spec_spec,
         ],
-        out_specs=[part_spec(5)] * groups,
-        out_shape=[jax.ShapeDtypeStruct((5, cap, narrow), BF)] * groups,
+        out_specs=[part_spec(PLANES)] * groups,
+        out_shape=[jax.ShapeDtypeStruct((PLANES, cap, narrow), BF)] * groups,
         scratch_shapes=[pltpu.VMEM((places, slots), BF)],
         compiler_params=params,
     )(counts, state_lower, state_gap, state_alpha, state_alpha, spec)
@@ -396,16 +429,12 @@
         compiler_params=params,
     )(counts, in_top, spec)
 
-    half = groups // 2
-    order = list(range(half, groups)) + list(range(near, half)) + list(range(1, near))
-    cut = [0, groups // 8, 3 * groups // 8, 5 * groups // 8, groups - 1]
     arrived = {0: pool[0]}
 
     def send_pool(stage, ready, *others):
-        parts = order[cut[stage] : cut[stage + 1]]
-        for k in parts:
+        for k in stages[stage]:
             arrived[k] = swap(after(pool[k], *others), k)
-        return after(ready, *[arrived[k] for k in parts])
+        return after(ready, *[arrived[k] for k in stages[stage]])
 
     held = {0: relaxed_top.reshape(2 * rows, narrow)}
     for b in reversed(range(bits)):
@@ -417,62 +446,91 @@
                 held[1] = swap(held[0], near)
                 held[1 << b] = after(held[1 << b], held[1], *near_panels)
     held[cores - 1] = send_pool(1, held[cores - 1], held[cores // 2])
-    partial = jnp.stack([dot(held[d], panel).astype(BF) for d in range(cores)])
-
-    for b in range(bits):
-        side = (core_pos >> b) & 1
-        half = partial.shape[0] // 2
-        keep = lax.dynamic_slice_in_dim(partial, side * half, half, 0)
-        give = lax.dynamic_slice_in_dim(partial, (1 - side) * half, half, 0)
-        taken = swap_core(give, 1 << b)
-        if b == bits - 1:
-            taken = send_pool(2, taken, give)
-        partial = (keep.astype(F32) + taken.astype(F32)).astype(BF)
+
     route = []
     for o in range(cores):
         for x in range(near):
             for c in range(cores):
                 to = o ^ bit_reverse(c, bits)
                 route.append(((o * near + x) * cores + c, (to * near + x) * cores + o))
-    coeff_low = lax.ppermute(partial[0], ("dom", "neu"), route)
-
-    coeff_low = send_pool(3, coeff_low, partial)
+
+    def product(rows_in):
+        return lax.optimization_barrier(dot(rows_in, panel).astype(BF))
+
+    def add(a, b):
+        return (a.astype(F32) + b.astype(F32)).astype(BF)
+
+    behind = [arrived[k] for k in range(1, near)]
+    sums = [product(after(held[d], *behind)) for d in range(cores)]
+    for b in range(bits):
+        low_side = ((core_pos >> b) & 1) == 0
+        count = len(sums) // 2
+        folded = []
+        for first, second in zip(sums[:count], sums[count:]):
+            give = jnp.where(low_side, second, first)
+            taken = swap_core(give, 1 << b)
+            if b == bits - 1:
+                taken = send_pool(2, taken, give)
+            folded.append(add(jnp.where(low_side, first, second), taken))
+        sums = folded
+    coeff_low = lax.ppermute(sums[0], ("dom", "neu"), route)
 
     hbm = pl.BlockSpec(memory_space=pl.ANY)
-    moved_lower, moved_gap, moved_alpha, offset = pl.pallas_call(
-        functools.partial(low_kernel, groups, cap),
+    parts = [arrived[k] for k in range(groups)]
+    moved_lower, moved_gap, moved_alpha = pl.pallas_call(
+        functools.partial(settle_kernel, groups, cap),
         grid=grid,
-        in_specs=[smem]
-        + [part_spec(5)] * groups
-        + [both_spec, whole(rows, TAGS), whole(rows, 2), flat_spec, spec_spec, hbm, hbm],
-        out_specs=[
-            plane_spec(0, rows),
-            plane_spec(0, rows),
-            pl.BlockSpec((2, rows, 2, tile), lambda i: (0, 0, 0, i)),
-            whole(rows, 2),
-        ],
+        in_specs=[smem] + [part_spec(LOW_PLANES)] * groups + [hbm, hbm],
+        out_specs=[plane_spec(0, rows), plane_spec(0, rows), pair_spec(0, rows)],
         out_shape=[
             jax.ShapeDtypeStruct((2, rows, narrow), BF),
             jax.ShapeDtypeStruct((2, rows, narrow), BF),
             jax.ShapeDtypeStruct((2, rows, 2, narrow), BF),
-            jax.ShapeDtypeStruct((rows, 2), F32),
-        ],
-        input_output_aliases={groups + 6: 0, groups + 7: 1},
+        ],
+        input_output_aliases={groups + 1: 0, groups + 2: 1},
         scratch_shapes=[pltpu.VMEM((rows, places), BF)],
         compiler_params=params,
+    )(counts, *parts, moved_lower, moved_gap)
+
+    rest_spec = pl.BlockSpec((1, cap, tile), lambda i: (LOW_PLANES, 0, i))
+    moved_alpha = pl.pallas_call(
+        functools.partial(rest_kernel, groups, cap),
+        grid=grid,
+        in_specs=[smem] + [rest_spec] * groups + [flat_spec, spec_spec, hbm],
+        out_specs=pair_spec(1, rows),
+        out_shape=jax.ShapeDtypeStruct((2, rows, 2, narrow), BF),
+        input_output_aliases={groups + 3: 0},
+        scratch_shapes=[pltpu.VMEM((rows, places), BF)],
+        compiler_params=params,
+    )(counts, *parts, used_top, spec, moved_alpha)
+
+    offset = pl.pallas_call(
+        low_kernel,
+        grid=grid,
+        in_specs=[
+            both_spec,
+            whole(rows, TAGS),
+            whole(rows, 2),
+            plane_spec(0, rows),
+            plane_spec(0, rows),
+            pair_spec(0, rows),
+        ],
+        out_specs=whole(rows, 2),
+        out_shape=jax.ShapeDtypeStruct((rows, 2), F32),
+        compiler_params=params,
     )(
-        counts,
-        *[arrived[k] for k in range(groups)],
         coeff_low.reshape(2, rows, narrow),
         moved_tags,
         offset,
-        used_top,
-        spec,
         moved_lower,
         moved_gap,
+        moved_alpha,
     )
 
-    totals = lax.psum(offset, "neu")
+    terms = [offset] + [swap_core(offset, c) for c in range(1, cores)]
+    while len(terms) > 1:
+        terms = [a + b for a, b in zip(terms[0::2], terms[1::2])]
+    totals = terms[0]
     bounds = jnp.stack([totals[:, 0], -totals[:, 1]], axis=1)
     neuron_ids = moved_tags[:, 0].astype(I32) * 128 + moved_tags[:, 1].astype(I32)
     sign_ids = moved_tags[:, 2].astype(I32)

time: 490 us -> 451 us (0.920)
  waiting for transfers between devices: 334 us -> 298 us
  blocking collectives: 21.7 us -> 0 us
  starting transfers between devices: 44.2 us -> 60.1 us
  Pallas kernels: 38.7 us -> 44.9 us
    ppermute x11, waiting for transfers between devices: 232 us -> 198 us  [swap(): return lax.ppermute(value, 'dom', [(d, d ^ mask) for d in range(groups)])]
    ppermute x2 -> x6, starting transfers between devices: 1.55 us -> 28 us  [swap_core(): return lax.ppermute(value, 'neu', [(c, c ^ mask) for c in range(cores)])]
    psum x1 -> x0, blocking collectives: 21.7 us -> none  [shards(): totals = lax.psum(offset, 'neu')]
    ppermute x1, starting transfers between devices: 13.3 us -> 0.76 us  [shards(): coeff_low = lax.ppermute(sums[0], ('dom', 'neu'), route)]
    select_n x0 -> x3, other arithmetic: none -> 8.5 us  [shards(): give = jnp.where(low_side, second, first)]
    convert_element_type x2 -> x1, other arithmetic: 7.87 us -> 0.94 us  [add(): return (a.astype(F32) + b.astype(F32)).astype(BF)]
    pallas_call x1 -> x3, Pallas kernels: 9.87 us -> 16.5 us  [the longest x1 6.51 us: shards(): pl.pallas_call(low_kernel, grid=grid, in_specs=[both_spec, whole(rows, TA...]
    unnamed x19 -> x68, local copies, waits for them, and re-layouts: 8.91 us -> 13.4 us
  transfers between devices with their start and end apart: 15 -> 19, of which waited for: 8 -> 10; matrix products, arithmetic and copies ran while one was open for 4% -> 5% of each run, Pallas kernels for 4% -> 7%
where the time goes in v3:
time: 451 us
  waiting for transfers between devices  298 us (66%)
  starting transfers between devices  60.1 us (13%)
  Pallas kernels  44.9 us (10%)
  other arithmetic  16.1 us (4%)
  matrix products  15.2 us (3%)
  local copies, waits for them, and re-layouts  15 us (3%)
    ppermute x11, waiting for transfers between devices, swap(): return lax.ppermute(value, 'dom', [(d, d ^ mask) for d in range(groups)])  198 us
    all_to_all x1, waiting for transfers between devices, shards(): lax.all_to_all(packed_top, 'dom', split_axis=0, concat_axis=0, tiled=True)  92.9 us
    ppermute x6, starting transfers between devices, swap_core(): return lax.ppermute(value, 'neu', [(c, c ^ mask) for c in range(cores)])  28 us
    ppermute x11, starting transfers between devices, swap(): return lax.ppermute(value, 'dom', [(d, d ^ mask) for d in range(groups)])  23.9 us
    dot_general x4, matrix products, dot(): return jnp.dot(a, b, preferred_element_type=F32)  15.2 us
    pallas_call x1, Pallas kernels, shards(): pl.pallas_call(functools.partial(pool_pack_kernel, groups, cap), grid=gri...  14.3 us
    unnamed x68, local copies, waits for them, and re-layouts  13.4 us
  transfers between devices with their start and end apart: 19, of which 10 were waited for; matrix products, arithmetic and copies ran while one was open for 5% of the time, Pallas kernels for 7%

profile of v3, /device:TPU:0, one launch (start us, length us, event | category | flops | bytes accessed | tf_op | source)
XLA Modules:
  0.0 450.5 jit_solution(16491233697983961574)
XLA Ops:
  3.4 1.9 copy-done
  6.0 8.1 %shard_map.144 = bf16[8,152,2048]{2,1,0:T(8,128)(2,1)} custom-call(s32[8,8]{1,0:T(8,128)S(1)} %copy-done.13, bf16[8,384]{1,0:T(8,128)(2,1)S(1)} %concatenate.6.tags_ref, bf16[2,384,2048]{2,1,0:T(8,128)(2,1)S(1)} %copy-done, bf16[2,384,2048]{2,1,0:T(8,128)(2,1)} %refs_1_.3, bf16[2,384,2,2048]{3,2,1,0:T(2,128)(2,1)} %refs_3_.1, ...), custom_call_target="tpu_custom_call" | custom-call | tf_op jit(solution)/shard_map/pallas_call | solution.py:352
  14.1 7.4 %all-to-all-start = ((bf16[8,152,2048]{2,1,0:T(8,128)(2,1)}), bf16[8,152,2048]{2,1,0:T(8,128)(2,1)}, u32[]{:S(2)}, u32[]{:S(2)}) async-start(bf16[8,152,2048]{2,1,0:T(8,128)(2,1)} %shard_map.144), calls=%async_computation | async-start | bytes 9961472 | tf_op jit(solution)/shard_map/all_to_all | solution.py:368
  21.5 14.3 %shard_map.145 = (bf16[5,48,2048]{2,1,0:T(8,128)(2,1)S(1)}, bf16[5,48,2048]{2,1,0:T(8,128)(2,1)}, bf16[5,48,2048]{2,1,0:T(8,128)(2,1)}, bf16[5,48,2048]{2,1,0:T(...) custom-call(s32[8,8]{1,0:T(8,128)S(1)} %copy-done.14, ...), custom_call_target="tpu_custom_call" | custom-call | tf_op jit(solution)/shard_map/pallas_call | solution.py:378
  38.8 92.9 %all-to-all-done.in_ref = bf16[8,152,2048]{2,1,0:T(8,128)(2,1)} async-done(((bf16[8,152,2048]{2,1,0:T(8,128)(2,1)}), bf16[8,152,2048]{2,1,0:T(8,128)(2,1)}, u32[]{:S(2)}, u32[]{:S(2)}) %all-to-all-start) | async-done | bytes 4980768 | tf_op jit(solution)/shard_map/all_to_all | solution.py:368
  133.1 6.0 %shard_map.146 = (bf16[2,192,2048]{2,1,0:T(8,128)(2,1)}, bf16[2,192,2048]{2,1,0:T(8,128)(2,1)}, bf16[192,2048]{1,0:T(8,128)(2,1)S(1)}, bf16[2,192,2048]{2,1,0:T(...) custom-call(s32[8,8]{1,0:T(8,128)S(1)} %copy-done.14, bf16[8,152,2048]{2,1,0:T(8,128)(2,1)} %all-to-all-done.in_ref, ...), custom_call_target="tpu_custom_call" | custom-call | tf_op jit(solution)/shard_map/pallas_call | solution.py:408
  140.0 2.0 collective-permute-start.3
  142.0 2.9 collective-permute-start.1
  144.9 106.9 %collective-permute-done.2.refs_2_ = bf16[5,48,2048]{2,1,0:T(8,128)(2,1)S(1)} collective-permute-done((bf16[5,48,2048]{2,1,0:T(8,128)(2,1)}, bf16[5,48,2048]{2,1,0:T(8,128)(2,1)S(1)}, u32[]{:S(2)}, u32[]{:S(2)}) %collective-permute-start.2) | collective-permute-done | bytes 983072 | tf_op jit(solution)/shard_map/ppermute | solution.py:332
  255.9 1.8 collective-permute-start.7
  257.7 2.3 collective-permute-start.8
  260.0 3.8 broadcast_select_fusion.1
  263.8 34.4 %collective-permute-done.5.refs_1_ = bf16[5,48,2048]{2,1,0:T(8,128)(2,1)} collective-permute-done((bf16[5,48,2048]{2,1,0:T(8,128)(2,1)}, bf16[5,48,2048]{2,1,0:T(8,128)(2,1)}, u32[]{:S(2)}, u32[]{:S(2)}) %collective-permute-start.5) | collective-permute-done | bytes 983072 | tf_op jit(solution)/shard_map/ppermute | solution.py:332
  298.2 3.8 convolution_convert_fusion.3
  302.0 3.8 convolution_convert_fusion.1
  305.9 3.8 convolution_convert_fusion
  309.7 1.5 broadcast_select_fusion.2
  312.2 20.2 %collective-permute-done.8.refs_7_ = bf16[5,48,2048]{2,1,0:T(8,128)(2,1)S(1)} collective-permute-done((bf16[5,48,2048]{2,1,0:T(8,128)(2,1)}, bf16[5,48,2048]{2,1,0:T(8,128)(2,1)S(1)}, u32[]{:S(2)}, u32[]{:S(2)}) %collective-permute-start.8) | collective-permute-done | bytes 983072 | tf_op jit(solution)/shard_map/ppermute | solution.py:332
  332.4 3.8 convolution_convert_fusion.2
  337.9 3.7 collective-permute-done.9
  341.7 5.5 %broadcast_select_fusion.4 = (bf16[384,2048]{1,0:T(8,128)(2,1)S(1)}, bf16[384,2048]{1,0:T(8,128)(2,1)S(1)}, bf16[384,2048]{1,0:T(8,128)(2,1)S(1)}) fusion(pred[]{:T(512)S(6)} %eq.9, bf16[384,2048]{1,0:T(8,128)(2,1)} %collective-permute-done.10, bf16[384,2048]{1,0:T(8,128)(2,1)} %copy-done.23, bf16[384,2048]{1,0:T(8,128)(2,1)} %copy-done.24, pred[]{:T(512)S(6)} %eq.10, ...), kind=kLoop, calls=%fused_computation.12 | loop fusion | flops 8650752 | bytes 14155778 | tf_op jit(solution)/shard_map/jit(_where)/select_n | solution.py:470
  347.2 1.6 collective-permute-start.13
  348.8 3.0 collective-permute-start.12
  351.8 8.7 %collective-permute-start.11 = (bf16[5,48,2048]{2,1,0:T(8,128)(2,1)S(1)}, bf16[5,48,2048]{2,1,0:T(8,128)(2,1)S(1)}, u32[]{:S(2)}, u32[]{:S(2)}) collective-permute-start(bf16[5,48,2048]{2,1,0:T(8,128)(2,1)S(1)} %copy-done.18), channel_id=1, source_target_pairs={{0,12},{4,8},{8,4},{12,0},{16,28},{20,24},{24,20},{28,16},{1,13},{... | collective-permute-start | bytes 2949128 | tf_op jit(solution)/shard_map/ppermute | solution.py:332
  360.5 14.7 %collective-permute-done.12.refs_6_ = bf16[5,48,2048]{2,1,0:T(8,128)(2,1)S(1)} collective-permute-done((bf16[5,48,2048]{2,1,0:T(8,128)(2,1)S(1)}, bf16[5,48,2048]{2,1,0:T(8,128)(2,1)S(1)}, u32[]{:S(2)}, u32[]{:S(2)}) %collective-permute-start.12) | collective-permute-done | bytes 983072 | tf_op jit(solution)/shard_map/ppermute | solution.py:332
  375.3 21.0 %collective-permute-done.11.refs_3_ = bf16[5,48,2048]{2,1,0:T(8,128)(2,1)S(1)} collective-permute-done((bf16[5,48,2048]{2,1,0:T(8,128)(2,1)S(1)}, bf16[5,48,2048]{2,1,0:T(8,128)(2,1)S(1)}, u32[]{:S(2)}, u32[]{:S(2)}) %collective-permute-start.11) | collective-permute-done | bytes 983072 | tf_op jit(solution)/shard_map/ppermute | solution.py:332
  398.0 5.5 %shard_map.147 = (bf16[2,192,2048]{2,1,0:T(8,128)(2,1)}, bf16[2,192,2048]{2,1,0:T(8,128)(2,1)}, bf16[2,192,2,2048]{3,2,1,0:T(2,128)(2,1)}) custom-call(s32[8,8]{1,0:T(8,128)S(1)} %copy-done.14, bf16[5,48,2048]{2,1,0:T(8,128)(2,1)S(1)} %get-tuple-element.57.refs_0_, ...), custom_call_target="tpu_custom_call", output_to_operand_aliasing={{0}: (9, {}), {1}: (10, {})} | custom-call | tf_op jit(solution)/shard_map/pallas_call | solution.py:480
  407.1 4.6 %shard_map.148.alpha_ref = bf16[2,192,2,2048]{3,2,1,0:T(2,128)(2,1)} custom-call(s32[8,8]{1,0:T(8,128)S(1)} %copy-done.14, bf16[5,48,2048]{2,1,0:T(8,128)(2,1)S(1)} %copy-done.4, bf16[5,48,2048]{2,1,0:T(8,128)(2,1)} %collective-permute-done.5.refs_1_, bf16[5,48,2048]{2,1,0:T(8,128)(2,1)S(1)} %copy-done.6, ...), custom_call_target="tpu_custom_call", output_to_operand_aliasing={{}: (11, {})} | custom-call | tf_op jit(solution)/shard_map/pallas_call | solution.py:496
  411.7 6.5 %shard_map.149 = f32[192,2]{1,0:T(8,128)S(1)} custom-call(bf16[2,192,2048]{2,1,0:T(8,128)(2,1)S(1)} %bitcast.7, f32[192,8]{1,0:T(8,128)S(1)} %get-tuple-element.88.tags_ref, f32[192,2]{1,0:T(8,128)S(1)} %get-tuple-element.90.before_ref, bf16[2,192,2048]{2,1,0:T(8,128)(2,1)S(1)} %copy-done.1, bf16[2,192,2048]{2,1,0:T(8,128)(2,1)S(1)} %copy-done.2, ...), custom_call_target="tpu_custom_call" | custom-call | tf_op jit(solution)/shard_map/pallas_call | solution.py:507
  418.2 24.8 %collective-permute-start.15 = (f32[192,2]{1,0:T(8,128)S(1)}, f32[192,2]{1,0:T(8,128)S(1)}, u32[]{:S(2)}, u32[]{:S(2)}) collective-permute-start(f32[192,2]{1,0:T(8,128)S(1)} %shard_map.149), channel_id=1, source_target_pairs={{0,1},{1,0},{2,3},{3,2},{4,5},{5,4},{6,7},{7,6},{8,9},{9,8},{10,11... | collective-permute-start | bytes 4616 | tf_op jit(solution)/shard_map/ppermute | solution.py:335
  443.0 1.5 collective-permute-start.16
  446.2 2.2 collective-permute-done.16
  (103 shorter events, 24.6 us)
Async XLA Ops:
  14.1 7.4 %copy-start.14 = (s32[8,8]{1,0:T(8,128)S(1)}, s32[8,8]{1,0:T(8,128)}, u32[]{:S(2)}) copy-start(s32[8,8]{1,0:T(8,128)} %counts_ref.9) | copy-start | bytes 772
  14.1 117.5 %all-to-all-start = ((bf16[8,152,2048]{2,1,0:T(8,128)(2,1)}), bf16[8,152,2048]{2,1,0:T(8,128)(2,1)}, u32[]{:S(2)}, u32[]{:S(2)}) async-start(bf16[8,152,2048]{2,1,0:T(8,128)(2,1)} %shard_map.144), calls=%async_computation | async-start | bytes 9961472 | tf_op jit(solution)/shard_map/all_to_all | solution.py:368
  38.8 359.2 %copy-start.3 = (bf16[5,48,2048]{2,1,0:T(8,128)(2,1)}, bf16[5,48,2048]{2,1,0:T(8,128)(2,1)S(1)}, u32[]{:S(2)}) copy-start(bf16[5,48,2048]{2,1,0:T(8,128)(2,1)S(1)} %get-tuple-element.57.refs_0_) | copy-start | bytes 2949124
  131.6 10.4 %copy-start.21 = (bf16[5,48,2048]{2,1,0:T(8,128)(2,1)S(1)}, bf16[5,48,2048]{2,1,0:T(8,128)(2,1)}, u32[]{:S(2)}) copy-start(bf16[5,48,2048]{2,1,0:T(8,128)(2,1)} %copy-done.20) | copy-start | bytes 2949124
  131.6 121.5 %collective-permute-start.4 = (bf16[2048,1024]{1,0:T(8,128)(2,1)}, bf16[2048,1024]{1,0:T(8,128)(2,1)}, u32[]{:S(2)}, u32[]{:S(2)}) collective-permute-start(bf16[2048,1024]{1,0:T(8,128)(2,1)} %param.17), channel_id=1, source_target_pairs={{0,4},{4,0},{8,12},{12,8},{16,20},{20,16},{24,28},{28,24},{1,5},{5... | collective-permute-start | bytes 12582920 | tf_op jit(solution)/shard_map/ppermute | solution.py:332
  139.9 111.9 %copy-start.15 = (bf16[2,192,2048]{2,1,0:T(8,128)(2,1)}, bf16[2,192,2048]{2,1,0:T(8,128)(2,1)S(1)}, u32[]{:S(2)}) copy-start(bf16[2,192,2048]{2,1,0:T(8,128)(2,1)S(1)} %get-tuple-element.60) | copy-start | bytes 4718596
  139.9 111.9 %collective-permute-start = (bf16[384,2048]{1,0:T(8,128)(2,1)S(1)}, bf16[384,2048]{1,0:T(8,128)(2,1)S(1)}, u32[]{:S(2)}, u32[]{:S(2)}) collective-permute-start(bf16[384,2048]{1,0:T(8,128)(2,1)S(1)} %bitcast.8), channel_id=1, source_target_pairs={{0,16},{4,20},{8,24},{12,28},{16,0},{20,4},{24,8},{28,12},{1,17},{... | collective-permute-start | bytes 4718600 | tf_op jit(solution)/shard_map/ppermute | solution.py:332
  140.0 111.9 %collective-permute-start.3 = (bf16[384,2048]{1,0:T(8,128)(2,1)S(1)}, bf16[384,2048]{1,0:T(8,128)(2,1)S(1)}, u32[]{:S(2)}, u32[]{:S(2)}) collective-permute-start(bf16[384,2048]{1,0:T(8,128)(2,1)S(1)} %bitcast.9), channel_id=1, source_target_pairs={{0,8},{4,12},{8,0},{12,4},{16,24},{20,28},{24,16},{28,20},{1,9},{5... | collective-permute-start | bytes 4718600 | tf_op jit(solution)/shard_map/ppermute | solution.py:332
  142.0 109.8 %collective-permute-start.2 = (bf16[5,48,2048]{2,1,0:T(8,128)(2,1)}, bf16[5,48,2048]{2,1,0:T(8,128)(2,1)S(1)}, u32[]{:S(2)}, u32[]{:S(2)}) collective-permute-start(bf16[5,48,2048]{2,1,0:T(8,128)(2,1)} %get-tuple-element.64), channel_id=1, source_target_pairs={{0,8},{4,12},{8,0},{12,4},{16,24},{20,28},{24,16},{28,20},{1,9},{5... | collective-permute-start | bytes 2949128 | tf_op jit(solution)/shard_map/ppermute | solution.py:332
  142.0 109.8 %collective-permute-start.1 = (bf16[5,48,2048]{2,1,0:T(8,128)(2,1)S(1)}, bf16[5,48,2048]{2,1,0:T(8,128)(2,1)S(1)}, u32[]{:S(2)}, u32[]{:S(2)}) collective-permute-start(bf16[5,48,2048]{2,1,0:T(8,128)(2,1)S(1)} %copy-done.21), channel_id=1, source_target_pairs={{0,16},{4,20},{8,24},{12,28},{16,0},{20,4},{24,8},{28,12},{1,17},{... | collective-permute-start | bytes 2949128 | tf_op jit(solution)/shard_map/ppermute | solution.py:332
  251.8 146.2 %copy-start.5 = (bf16[5,48,2048]{2,1,0:T(8,128)(2,1)}, bf16[5,48,2048]{2,1,0:T(8,128)(2,1)S(1)}, u32[]{:S(2)}) copy-start(bf16[5,48,2048]{2,1,0:T(8,128)(2,1)S(1)} %collective-permute-done.2.refs_2_) | copy-start | bytes 2949124
  251.8 146.2 %copy-start.7 = (bf16[5,48,2048]{2,1,0:T(8,128)(2,1)}, bf16[5,48,2048]{2,1,0:T(8,128)(2,1)S(1)}, u32[]{:S(2)}) copy-start(bf16[5,48,2048]{2,1,0:T(8,128)(2,1)S(1)} %collective-permute-done.1.refs_4_) | copy-start | bytes 2949124
  254.2 44.0 %collective-permute-start.5 = (bf16[5,48,2048]{2,1,0:T(8,128)(2,1)}, bf16[5,48,2048]{2,1,0:T(8,128)(2,1)}, u32[]{:S(2)}, u32[]{:S(2)}) collective-permute-start(bf16[5,48,2048]{2,1,0:T(8,128)(2,1)} %get-tuple-element.68), channel_id=1, source_target_pairs={{0,4},{4,0},{8,12},{12,8},{16,20},{20,16},{24,28},{28,24},{1,5},{5... | collective-permute-start | bytes 2949128 | tf_op jit(solution)/shard_map/ppermute | solution.py:332
  254.7 43.5 %copy-start.31 = (bf16[384,2048]{1,0:T(8,128)(2,1)S(1)}, bf16[384,2048]{1,0:T(8,128)(2,1)}, u32[]{:S(2)}) copy-start(bf16[384,2048]{1,0:T(8,128)(2,1)} %copy-done.30) | copy-start | bytes 4718596
  254.7 77.7 %collective-permute-start.6 = (bf16[384,2048]{1,0:T(8,128)(2,1)}, bf16[384,2048]{1,0:T(8,128)(2,1)S(1)}, u32[]{:S(2)}, u32[]{:S(2)}) collective-permute-start(bf16[384,2048]{1,0:T(8,128)(2,1)} %copy-done.28), channel_id=1, source_target_pairs={{0,8},{4,12},{8,0},{12,4},{16,24},{20,28},{24,16},{28,20},{1,9},{5... | collective-permute-start | bytes 4718600 | tf_op jit(solution)/shard_map/ppermute | solution.py:332
  255.9 56.3 %collective-permute-start.7 = (bf16[5,48,2048]{2,1,0:T(8,128)(2,1)}, bf16[5,48,2048]{2,1,0:T(8,128)(2,1)S(1)}, u32[]{:S(2)}, u32[]{:S(2)}) collective-permute-start(bf16[5,48,2048]{2,1,0:T(8,128)(2,1)} %copy-done.19), channel_id=1, source_target_pairs={{0,20},{4,16},{8,28},{12,24},{16,4},{20,0},{24,12},{28,8},{1,21},{... | collective-permute-start | bytes 2949128 | tf_op jit(solution)/shard_map/ppermute | solution.py:332
  257.7 74.7 %collective-permute-start.8 = (bf16[5,48,2048]{2,1,0:T(8,128)(2,1)}, bf16[5,48,2048]{2,1,0:T(8,128)(2,1)S(1)}, u32[]{:S(2)}, u32[]{:S(2)}) collective-permute-start(bf16[5,48,2048]{2,1,0:T(8,128)(2,1)} %get-tuple-element.74), channel_id=1, source_target_pairs={{0,28},{4,24},{8,20},{12,16},{16,12},{20,8},{24,4},{28,0},{1,29},{... | collective-permute-start | bytes 2949128 | tf_op jit(solution)/shard_map/ppermute | solution.py:332
  302.0 34.2 %copy-start.22 = (bf16[384,2048]{1,0:T(8,128)(2,1)}, bf16[384,2048]{1,0:T(8,128)(2,1)S(1)}, u32[]{:S(2)}) copy-start(bf16[384,2048]{1,0:T(8,128)(2,1)S(1)} %convolution_convert_fusion.3) | copy-start | bytes 4718596
  309.7 26.5 %copy-start.24 = (bf16[384,2048]{1,0:T(8,128)(2,1)}, bf16[384,2048]{1,0:T(8,128)(2,1)S(1)}, u32[]{:S(2)}) copy-start(bf16[384,2048]{1,0:T(8,128)(2,1)S(1)} %convolution_convert_fusion) | copy-start | bytes 4718596
  311.2 26.7 %collective-permute-start.10 = (bf16[384,2048]{1,0:T(8,128)(2,1)}, bf16[384,2048]{1,0:T(8,128)(2,1)}, u32[]{:S(2)}, u32[]{:S(2)}) collective-permute-start(bf16[384,2048]{1,0:T(8,128)(2,1)} %broadcast_select_fusion.2), channel_id=1, source_target_pairs={{0,1},{1,0},{2,3},{3,2},{4,5},{5,4},{6,7},{7,6},{8,9},{9,8},{10,11... | collective-permute-start | bytes 4718600 | tf_op jit(solution)/shard_map/ppermute | solution.py:335
  312.2 24.1 %copy-start.9 = (bf16[5,48,2048]{2,1,0:T(8,128)(2,1)}, bf16[5,48,2048]{2,1,0:T(8,128)(2,1)S(1)}, u32[]{:S(2)}) copy-start(bf16[5,48,2048]{2,1,0:T(8,128)(2,1)S(1)} %collective-permute-done.7.refs_5_) | copy-start | bytes 2949124
  337.9 3.8 collective-permute-start.9
  337.9 10.9 %copy-start.32 = (bf16[5,48,2048]{2,1,0:T(8,128)(2,1)S(1)}, bf16[5,48,2048]{2,1,0:T(8,128)(2,1)}, u32[]{:S(2)}) copy-start(bf16[5,48,2048]{2,1,0:T(8,128)(2,1)} %get-tuple-element.81) | copy-start | bytes 2949124
  337.9 13.9 %copy-start.18 = (bf16[5,48,2048]{2,1,0:T(8,128)(2,1)S(1)}, bf16[5,48,2048]{2,1,0:T(8,128)(2,1)}, u32[]{:S(2)}) copy-start(bf16[5,48,2048]{2,1,0:T(8,128)(2,1)} %copy-done.17) | copy-start | bytes 2949124
  347.2 49.0 %collective-permute-start.13 = (bf16[384,2048]{1,0:T(8,128)(2,1)S(1)}, bf16[384,2048]{1,0:T(8,128)(2,1)S(1)}, u32[]{:S(2)}, u32[]{:S(2)}) collective-permute-start(bf16[384,2048]{1,0:T(8,128)(2,1)S(1)} %get-tuple-element.121), channel_id=1, source_target_pairs={{0,2},{1,3},{2,0},{3,1},{4,6},{5,7},{6,4},{7,5},{8,10},{9,11},{10,... | collective-permute-start | bytes 4718600 | tf_op jit(solution)/shard_map/ppermute | solution.py:335
  348.8 26.5 %collective-permute-start.12 = (bf16[5,48,2048]{2,1,0:T(8,128)(2,1)S(1)}, bf16[5,48,2048]{2,1,0:T(8,128)(2,1)S(1)}, u32[]{:S(2)}, u32[]{:S(2)}) collective-permute-start(bf16[5,48,2048]{2,1,0:T(8,128)(2,1)S(1)} %copy-done.32), channel_id=1, source_target_pairs={{0,24},{4,28},{8,16},{12,20},{16,8},{20,12},{24,0},{28,4},{1,25},{... | collective-permute-start | bytes 2949128 | tf_op jit(solution)/shard_map/ppermute | solution.py:332
  351.8 44.4 %collective-permute-start.11 = (bf16[5,48,2048]{2,1,0:T(8,128)(2,1)S(1)}, bf16[5,48,2048]{2,1,0:T(8,128)(2,1)S(1)}, u32[]{:S(2)}, u32[]{:S(2)}) collective-permute-start(bf16[5,48,2048]{2,1,0:T(8,128)(2,1)S(1)} %copy-done.18), channel_id=1, source_target_pairs={{0,12},{4,8},{8,4},{12,0},{16,28},{20,24},{24,20},{28,16},{1,13},{... | collective-permute-start | bytes 2949128 | tf_op jit(solution)/shard_map/ppermute | solution.py:332
  375.3 21.9 %copy-start.27 = (bf16[5,48,2048]{2,1,0:T(8,128)(2,1)}, bf16[5,48,2048]{2,1,0:T(8,128)(2,1)S(1)}, u32[]{:S(2)}) copy-start(bf16[5,48,2048]{2,1,0:T(8,128)(2,1)S(1)} %collective-permute-done.12.refs_6_) | copy-start | bytes 2949124
  397.2 14.5 %collective-permute-start.14 = (bf16[384,2048]{1,0:T(8,128)(2,1)S(1)}, bf16[384,2048]{1,0:T(8,128)(2,1)S(1)}, u32[]{:S(2)}, u32[]{:S(2)}) collective-permute-start(bf16[384,2048]{1,0:T(8,128)(2,1)S(1)} %add_convert_fusion), channel_id=1, source_target_pairs={{0,0},{1,16},{2,8},{3,24},{4,4},{5,20},{6,12},{7,28},{8,9},{9,25},... | collective-permute-start | bytes 4718600 | tf_op jit(solution)/shard_map/ppermute | solution.py:476
  418.2 28.0 %collective-permute-start.15 = (f32[192,2]{1,0:T(8,128)S(1)}, f32[192,2]{1,0:T(8,128)S(1)}, u32[]{:S(2)}, u32[]{:S(2)}) collective-permute-start(f32[192,2]{1,0:T(8,128)S(1)} %shard_map.149), channel_id=1, source_target_pairs={{0,1},{1,0},{2,3},{3,2},{4,5},{5,4},{6,7},{7,6},{8,9},{9,8},{10,11... | collective-permute-start | bytes 4616 | tf_op jit(solution)/shard_map/ppermute | solution.py:335
  443.0 5.3 %collective-permute-start.16 = (f32[192,2]{1,0:T(8,128)S(1)}, f32[192,2]{1,0:T(8,128)S(1)}, u32[]{:S(2)}, u32[]{:S(2)}) collective-permute-start(f32[192,2]{1,0:T(8,128)S(1)} %shard_map.149), channel_id=1, source_target_pairs={{0,2},{1,3},{2,0},{3,1},{4,6},{5,7},{6,4},{7,5},{8,10},{9,11},{10,... | collective-permute-start | bytes 4616 | tf_op jit(solution)/shard_map/ppermute | solution.py:335
  444.6 5.1 %collective-permute-start.17 = (f32[192,2]{1,0:T(8,128)S(1)}, f32[192,2]{1,0:T(8,128)S(1)}, u32[]{:S(2)}, u32[]{:S(2)}) collective-permute-start(f32[192,2]{1,0:T(8,128)S(1)} %shard_map.149), channel_id=1, source_target_pairs={{0,3},{1,2},{2,1},{3,0},{4,7},{5,6},{6,5},{7,4},{8,11},{9,10},{10,... | collective-permute-start | bytes 4616 | tf_op jit(solution)/shard_map/ppermute | solution.py:335
  (20 other events, 45.8 us)

commit v4 on v3

--- a/solution.py
+++ b/solution.py
@@ -25,7 +25,7 @@
 
 
 def tile_of(narrow):
-    return min(512, narrow)
+    return min(1024, narrow)
 
 
 def dot(a, b):
@@ -101,7 +101,7 @@
             out_refs[k][p] = packed[k]
 
 
-def top_pack_kernel(groups, cap, counts_ref, tags_ref, *refs):
+def top_pack_kernel(groups, cap, counts_ref, neuron_ref, sign_ref, beta_ref, *refs):
     sources, out_ref, mat_ref = refs[:-2], refs[-2], refs[-1]
     slots = mat_ref.shape[1]
 
@@ -109,11 +109,24 @@
     def _():
         mat_ref[...] = send_matrix(counts_ref, False, groups, cap, slots)
         me = lax.axis_index("dom")
+        neuron, beta = neuron_ref[...], beta_ref[...].astype(F32)
+        facts = [
+            (neuron >> 7).astype(F32),
+            (neuron & 127).astype(F32),
+            sign_ref[...].astype(F32),
+            beta[0:1],
+            beta[1:2],
+        ]
+        line = lax.broadcasted_iota(I32, (TAGS, slots), 0)
+        tags = jnp.zeros((TAGS, slots), F32)
+        for t, fact in enumerate(facts):
+            tags = jnp.where(line == t, fact, tags)
+        tags = tags.astype(BF)
         place = lax.broadcasted_iota(I32, (LANES, slots), 0)
         slot = lax.broadcasted_iota(I32, (LANES, slots), 1)
         for e in range(groups):
             hit = (slot == place + prefix(counts_ref, me, e, groups)).astype(BF)
-            out_ref[e, 3 * cap :, 0:LANES] = dot_nt(tags_ref[...], hit).astype(BF)
+            out_ref[e, 3 * cap :, 0:LANES] = dot_nt(tags, hit).astype(BF)
 
     mat = mat_ref[...]
     for p, plane in enumerate(top_planes(*sources)):
@@ -253,7 +266,9 @@
     alpha_ref[0, :, 1, :] = either(spec_ref, rest, used)
 
 
-def low_kernel(coeff_ref, tags_ref, before_ref, lower_ref, gap_ref, alpha_ref, offset_ref):
+def low_kernel(
+    first_ref, second_ref, tags_ref, before_ref, lower_ref, gap_ref, alpha_ref, offset_ref
+):
     rows, tile = lower_ref.shape[1:]
     step = pl.program_id(0)
     narrow = tile * pl.num_programs(0)
@@ -271,7 +286,7 @@
     sums = []
     for s in range(2):
         alpha = alpha_ref[0, :, s, :].astype(F32)
-        coeff = coeff_ref[s].astype(F32)
+        coeff = (first_ref, second_ref)[s][...].astype(F32)
         lower_slope = lower_slope_of(alpha, active, inactive, chosen, split_slope)
         negative = jnp.minimum(coeff, 0.0)
         value = jnp.maximum(coeff, 0.0) * lower_slope + negative * upper_slope
@@ -337,16 +352,6 @@
     def after(value, *others):
         return lax.optimization_barrier((value,) + others)[0]
 
-    tags = jnp.concatenate(
-        [
-            (split_neuron >> 7).astype(BF)[None],
-            (split_neuron & 127).astype(BF)[None],
-            split_sign.astype(BF)[None],
-            split_beta.T,
-            jnp.zeros((TAGS - 5, slots), BF),
-        ],
-        axis=0,
-    )
     top_rows = 3 * cap + TAGS
     top_spec = pl.BlockSpec((groups, top_rows, tile), lambda i: (0, 0, i))
     packed_top = pl.pallas_call(
@@ -354,7 +359,9 @@
         grid=grid,
         in_specs=[
             smem,
-            whole(TAGS, slots),
+            whole(1, slots),
+            whole(1, slots),
+            whole(2, slots),
             plane_spec(1, slots),
             plane_spec(1, slots),
             pair_spec(1, slots),
@@ -364,7 +371,16 @@
         out_shape=jax.ShapeDtypeStruct((groups, top_rows, narrow), BF),
         scratch_shapes=[pltpu.VMEM((places, slots), BF)],
         compiler_params=params,
-    )(counts, tags, state_lower, state_gap, state_alpha, spec)
+    )(
+        counts,
+        split_neuron[None],
+        split_sign[None],
+        split_beta.T,
+        state_lower,
+        state_gap,
+        state_alpha,
+        spec,
+    )
     in_top = lax.all_to_all(packed_top, "dom", split_axis=0, concat_axis=0, tiled=True)
 
     half, quarter = groups // 2, groups // 8
@@ -462,18 +478,27 @@
 
     behind = [arrived[k] for k in range(1, near)]
     sums = [product(after(held[d], *behind)) for d in range(cores)]
-    for b in range(bits):
+    for b in range(bits - 1):
         low_side = ((core_pos >> b) & 1) == 0
         count = len(sums) // 2
         folded = []
         for first, second in zip(sums[:count], sums[count:]):
-            give = jnp.where(low_side, second, first)
-            taken = swap_core(give, 1 << b)
-            if b == bits - 1:
-                taken = send_pool(2, taken, give)
+            taken = swap_core(jnp.where(low_side, second, first), 1 << b)
             folded.append(add(jnp.where(low_side, first, second), taken))
-        sums = folded
-    coeff_low = lax.ppermute(sums[0], ("dom", "neu"), route)
+        sums = [lax.optimization_barrier(value) for value in folded[:-1]] + folded[-1:]
+
+    low_side = ((core_pos >> (bits - 1)) & 1) == 0
+    gives = jnp.where(low_side, sums[1], sums[0])
+    keeps = jnp.where(low_side, sums[0], sums[1])
+    coeff = []
+    taken = gives
+    for s in range(2):
+        half_rows = slice(s * rows, (s + 1) * rows)
+        taken = swap_core(after(gives[half_rows], taken), 1 << (bits - 1))
+        if s == 1:
+            taken = send_pool(2, taken, gives)
+        value = add(keeps[half_rows], taken)
+        coeff.append(lax.ppermute(value, ("dom", "neu"), route))
 
     hbm = pl.BlockSpec(memory_space=pl.ANY)
     parts = [arrived[k] for k in range(groups)]
@@ -508,7 +533,8 @@
         low_kernel,
         grid=grid,
         in_specs=[
-            both_spec,
+            flat_spec,
+            flat_spec,
             whole(rows, TAGS),
             whole(rows, 2),
             plane_spec(0, rows),
@@ -519,7 +545,7 @@
         out_shape=jax.ShapeDtypeStruct((rows, 2), F32),
         compiler_params=params,
     )(
-        coeff_low.reshape(2, rows, narrow),
+        *coeff,
         moved_tags,
         offset,
         moved_lower,
@@ -531,7 +557,7 @@
     while len(terms) > 1:
         terms = [a + b for a, b in zip(terms[0::2], terms[1::2])]
     totals = terms[0]
-    bounds = jnp.stack([totals[:, 0], -totals[:, 1]], axis=1)
+    bounds = totals * jnp.array([1.0, -1.0], dtype=F32)
     neuron_ids = moved_tags[:, 0].astype(I32) * 128 + moved_tags[:, 1].astype(I32)
     sign_ids = moved_tags[:, 2].astype(I32)
     moved_beta = moved_tags[:, 3:5].astype(BF)

time: 451 us -> 447 us (level)
  waiting for transfers between devices: 298 us -> 293 us
    ppermute x11, waiting for transfers between devices: 198 us -> 190 us  [swap(): return lax.ppermute(value, 'dom', [(d, d ^ mask) for d in range(groups)])]
    ppermute x6 -> x7, waiting for transfers between devices: 7.2 us -> 10.8 us  [swap_core(): return lax.ppermute(value, 'neu', [(c, c ^ mask) for c in range(cores)])]
    ppermute x6 -> x7, starting transfers between devices: 28 us -> 30.5 us  [swap_core(): return lax.ppermute(value, 'neu', [(c, c ^ mask) for c in range(cores)])]
    unnamed x68 -> x76, local copies, waits for them, and re-layouts: 13.4 us -> 14.7 us
  transfers between devices with their start and end apart: 19 -> 21, of which waited for: 10 -> 11; matrix products, arithmetic and copies ran while one was open for 5% -> 6% of each run, Pallas kernels for 7% -> 7%
where the time goes in v4:
time: 447 us
  waiting for transfers between devices  293 us (66%)
  starting transfers between devices  63.2 us (14%)
  Pallas kernels  43.1 us (10%)
  local copies, waits for them, and re-layouts  17 us (4%)
  matrix products  15.4 us (3%)
  other arithmetic  14 us (3%)
    ppermute x11, waiting for transfers between devices, swap(): return lax.ppermute(value, 'dom', [(d, d ^ mask) for d in range(groups)])  190 us
    all_to_all x1, waiting for transfers between devices, shards(): lax.all_to_all(packed_top, 'dom', split_axis=0, concat_axis=0, tiled=True)  92.1 us
    ppermute x7, starting transfers between devices, swap_core(): return lax.ppermute(value, 'neu', [(c, c ^ mask) for c in range(cores)])  30.5 us
    ppermute x11, starting transfers between devices, swap(): return lax.ppermute(value, 'dom', [(d, d ^ mask) for d in range(groups)])  23.9 us
    dot_general x4, matrix products, dot(): return jnp.dot(a, b, preferred_element_type=F32)  15.4 us
    pallas_call x1, Pallas kernels, shards(): pl.pallas_call(functools.partial(pool_pack_kernel, groups, cap), grid=gri...  15.1 us
    unnamed x76, local copies, waits for them, and re-layouts  14.7 us
    ppermute x7, waiting for transfers between devices, swap_core(): return lax.ppermute(value, 'neu', [(c, c ^ mask) for c in range(cores)])  10.8 us
  transfers between devices with their start and end apart: 21, of which 11 were waited for; matrix products, arithmetic and copies ran while one was open for 6% of the time, Pallas kernels for 7%

profile of v4, /device:TPU:0, one launch (start us, length us, event | category | flops | bytes accessed | tf_op | source)
XLA Modules:
  0.0 446.8 jit_solution(16383462749351010119)
XLA Ops:
  2.7 1.9 copy-done
  6.0 8.0 %shard_map.153 = bf16[8,152,2048]{2,1,0:T(8,128)(2,1)} custom-call(s32[8,8]{1,0:T(8,128)S(1)} %copy-done.13, s32[1,384]{1,0:T(1,128)S(1)} %broadcast_in_dim.10.neuron_ref, s32[1,384]{1,0:T(1,128)S(1)} %broadcast_in_dim.11.sign_ref, bf16[2,384]{1,0:T(2,128)(2,1)S(1)} %bitcast.6, bf16[2,384,2048]{2,1,0:T(8,128)(2,1)S(1)} %copy-done, ...), custom_call_target="tpu_custom_call" | custom-call | tf_op jit(solution)/shard_map/pallas_call | solution.py:357
  13.9 7.4 %all-to-all-start = ((bf16[8,152,2048]{2,1,0:T(8,128)(2,1)}), bf16[8,152,2048]{2,1,0:T(8,128)(2,1)}, u32[]{:S(2)}, u32[]{:S(2)}) async-start(bf16[8,152,2048]{2,1,0:T(8,128)(2,1)} %shard_map.153), calls=%async_computation | async-start | bytes 9961472 | tf_op jit(solution)/shard_map/all_to_all | solution.py:384
  21.3 15.1 %shard_map.154 = (bf16[5,48,2048]{2,1,0:T(8,128)(2,1)S(1)}, bf16[5,48,2048]{2,1,0:T(8,128)(2,1)}, bf16[5,48,2048]{2,1,0:T(8,128)(2,1)}, bf16[5,48,2048]{2,1,0:T(...) custom-call(s32[8,8]{1,0:T(8,128)S(1)} %copy-done.14, ...), custom_call_target="tpu_custom_call" | custom-call | tf_op jit(solution)/shard_map/pallas_call | solution.py:394
  39.4 92.1 %all-to-all-done.in_ref = bf16[8,152,2048]{2,1,0:T(8,128)(2,1)} async-done(((bf16[8,152,2048]{2,1,0:T(8,128)(2,1)}), bf16[8,152,2048]{2,1,0:T(8,128)(2,1)}, u32[]{:S(2)}, u32[]{:S(2)}) %all-to-all-start) | async-done | bytes 4980768 | tf_op jit(solution)/shard_map/all_to_all | solution.py:384
  132.9 5.6 %shard_map.155 = (bf16[2,192,2048]{2,1,0:T(8,128)(2,1)}, bf16[2,192,2048]{2,1,0:T(8,128)(2,1)}, bf16[192,2048]{1,0:T(8,128)(2,1)S(1)}, bf16[2,192,2048]{2,1,0:T(...) custom-call(s32[8,8]{1,0:T(8,128)S(1)} %copy-done.14, bf16[8,152,2048]{2,1,0:T(8,128)(2,1)} %all-to-all-done.in_ref, ...), custom_call_target="tpu_custom_call" | custom-call | tf_op jit(solution)/shard_map/pallas_call | solution.py:424
  139.4 2.0 collective-permute-start.3
  141.4 2.9 collective-permute-start.1
  144.3 106.9 %collective-permute-done.2.refs_2_ = bf16[5,48,2048]{2,1,0:T(8,128)(2,1)S(1)} collective-permute-done((bf16[5,48,2048]{2,1,0:T(8,128)(2,1)}, bf16[5,48,2048]{2,1,0:T(8,128)(2,1)S(1)}, u32[]{:S(2)}, u32[]{:S(2)}) %collective-permute-start.2) | collective-permute-done | bytes 983072 | tf_op jit(solution)/shard_map/ppermute | solution.py:347
  255.3 1.8 collective-permute-start.7
  257.1 2.3 collective-permute-start.8
  259.4 3.8 broadcast_select_fusion.1
  263.2 34.4 %collective-permute-done.5.refs_1_ = bf16[5,48,2048]{2,1,0:T(8,128)(2,1)} collective-permute-done((bf16[5,48,2048]{2,1,0:T(8,128)(2,1)}, bf16[5,48,2048]{2,1,0:T(8,128)(2,1)}, u32[]{:S(2)}, u32[]{:S(2)}) %collective-permute-start.5) | collective-permute-done | bytes 983072 | tf_op jit(solution)/shard_map/ppermute | solution.py:347
  297.6 3.8 convolution_convert_fusion.3
  301.4 3.8 convolution_convert_fusion.1
  305.3 4.0 convolution_convert_fusion
  311.6 20.3 %collective-permute-done.8.refs_7_ = bf16[5,48,2048]{2,1,0:T(8,128)(2,1)S(1)} collective-permute-done((bf16[5,48,2048]{2,1,0:T(8,128)(2,1)}, bf16[5,48,2048]{2,1,0:T(8,128)(2,1)S(1)}, u32[]{:S(2)}, u32[]{:S(2)}) %collective-permute-start.8) | collective-permute-done | bytes 983072 | tf_op jit(solution)/shard_map/ppermute | solution.py:347
  331.8 3.8 convolution_convert_fusion.2
  337.3 2.9 add_convert_fusion
  341.1 2.8 broadcast_select_fusion.4
  344.2 1.6 collective-permute-start.13
  345.8 3.0 collective-permute-start.12
  348.8 8.7 %collective-permute-start.11 = (bf16[5,48,2048]{2,1,0:T(8,128)(2,1)S(1)}, bf16[5,48,2048]{2,1,0:T(8,128)(2,1)S(1)}, u32[]{:S(2)}, u32[]{:S(2)}) collective-permute-start(bf16[5,48,2048]{2,1,0:T(8,128)(2,1)S(1)} %copy-done.19), channel_id=1, source_target_pairs={{0,12},{4,8},{8,4},{12,0},{16,28},{20,24},{24,20},{28,16},{1,13},{... | collective-permute-start | bytes 2949128 | tf_op jit(solution)/shard_map/ppermute | solution.py:347
  357.5 6.4 %collective-permute-done.13 = bf16[192,2048]{1,0:T(8,128)(2,1)S(1)} collective-permute-done((bf16[192,2048]{1,0:T(8,128)(2,1)S(1)}, bf16[192,2048]{1,0:T(8,128)(2,1)S(1)}, u32[]{:S(2)}, u32[]{:S(2)}) %collective-permute-start.13) | collective-permute-done | bytes 786464 | tf_op jit(solution)/shard_map/ppermute | solution.py:350
  365.4 6.9 %collective-permute-done.12.refs_6_ = bf16[5,48,2048]{2,1,0:T(8,128)(2,1)S(1)} collective-permute-done((bf16[5,48,2048]{2,1,0:T(8,128)(2,1)S(1)}, bf16[5,48,2048]{2,1,0:T(8,128)(2,1)S(1)}, u32[]{:S(2)}, u32[]{:S(2)}) %collective-permute-start.12) | collective-permute-done | bytes 983072 | tf_op jit(solution)/shard_map/ppermute | solution.py:347
  372.3 21.0 %collective-permute-done.11.refs_3_ = bf16[5,48,2048]{2,1,0:T(8,128)(2,1)S(1)} collective-permute-done((bf16[5,48,2048]{2,1,0:T(8,128)(2,1)S(1)}, bf16[5,48,2048]{2,1,0:T(8,128)(2,1)S(1)}, u32[]{:S(2)}, u32[]{:S(2)}) %collective-permute-start.11) | collective-permute-done | bytes 983072 | tf_op jit(solution)/shard_map/ppermute | solution.py:347
  395.4 5.0 %shard_map.156 = (bf16[2,192,2048]{2,1,0:T(8,128)(2,1)}, bf16[2,192,2048]{2,1,0:T(8,128)(2,1)}, bf16[2,192,2,2048]{3,2,1,0:T(2,128)(2,1)}) custom-call(s32[8,8]{1,0:T(8,128)S(1)} %copy-done.14, bf16[5,48,2048]{2,1,0:T(8,128)(2,1)S(1)} %get-tuple-element.59.refs_0_, ...), custom_call_target="tpu_custom_call", output_to_operand_aliasing={{0}: (9, {}), {1}: (10, {})} | custom-call | tf_op jit(solution)/shard_map/pallas_call | solution.py:505
  404.0 3.5 shard_map.157.alpha_ref
  407.5 6.1 %shard_map.158 = f32[192,2]{1,0:T(8,128)S(1)} custom-call(bf16[192,2048]{1,0:T(8,128)(2,1)S(1)} %collective-permute-done.14.first_ref, bf16[192,2048]{1,0:T(8,128)(2,1)S(1)} %collective-permute-done.16.second_ref, f32[192,8]{1,0:T(8,128)S(1)} %get-tuple-element.90.tags_ref, f32[192,2]{1,0:T(8,128)S(1)} %get-tuple-element.94.before_ref, ...), custom_call_target="tpu_custom_call" | custom-call | tf_op jit(solution)/shard_map/pallas_call | solution.py:532
  413.6 25.1 %collective-permute-start.17 = (f32[192,2]{1,0:T(8,128)S(1)}, f32[192,2]{1,0:T(8,128)S(1)}, u32[]{:S(2)}, u32[]{:S(2)}) collective-permute-start(f32[192,2]{1,0:T(8,128)S(1)} %shard_map.158), channel_id=1, source_target_pairs={{0,1},{1,0},{2,3},{3,2},{4,5},{5,4},{6,7},{7,6},{8,9},{9,8},{10,11... | collective-permute-start | bytes 4616 | tf_op jit(solution)/shard_map/ppermute | solution.py:350
  438.7 2.2 collective-permute-start.18
  442.5 2.0 collective-permute-done.18
  (110 shorter events, 28.9 us)
Async XLA Ops:
  13.9 117.5 %all-to-all-start = ((bf16[8,152,2048]{2,1,0:T(8,128)(2,1)}), bf16[8,152,2048]{2,1,0:T(8,128)(2,1)}, u32[]{:S(2)}, u32[]{:S(2)}) async-start(bf16[8,152,2048]{2,1,0:T(8,128)(2,1)} %shard_map.153), calls=%async_computation | async-start | bytes 9961472 | tf_op jit(solution)/shard_map/all_to_all | solution.py:384
  39.4 356.0 %copy-start.3 = (bf16[5,48,2048]{2,1,0:T(8,128)(2,1)}, bf16[5,48,2048]{2,1,0:T(8,128)(2,1)S(1)}, u32[]{:S(2)}) copy-start(bf16[5,48,2048]{2,1,0:T(8,128)(2,1)S(1)} %get-tuple-element.59.refs_0_) | copy-start | bytes 2949124
  131.5 121.0 %collective-permute-start.4 = (bf16[2048,1024]{1,0:T(8,128)(2,1)}, bf16[2048,1024]{1,0:T(8,128)(2,1)}, u32[]{:S(2)}, u32[]{:S(2)}) collective-permute-start(bf16[2048,1024]{1,0:T(8,128)(2,1)} %param.18), channel_id=1, source_target_pairs={{0,4},{4,0},{8,12},{12,8},{16,20},{20,16},{24,28},{28,24},{1,5},{5... | collective-permute-start | bytes 12582920 | tf_op jit(solution)/shard_map/ppermute | solution.py:347
  139.4 111.9 %copy-start.16 = (bf16[2,192,2048]{2,1,0:T(8,128)(2,1)}, bf16[2,192,2048]{2,1,0:T(8,128)(2,1)S(1)}, u32[]{:S(2)}) copy-start(bf16[2,192,2048]{2,1,0:T(8,128)(2,1)S(1)} %get-tuple-element.62) | copy-start | bytes 4718596
  139.4 111.9 %collective-permute-start = (bf16[384,2048]{1,0:T(8,128)(2,1)S(1)}, bf16[384,2048]{1,0:T(8,128)(2,1)S(1)}, u32[]{:S(2)}, u32[]{:S(2)}) collective-permute-start(bf16[384,2048]{1,0:T(8,128)(2,1)S(1)} %bitcast.7), channel_id=1, source_target_pairs={{0,16},{4,20},{8,24},{12,28},{16,0},{20,4},{24,8},{28,12},{1,17},{... | collective-permute-start | bytes 4718600 | tf_op jit(solution)/shard_map/ppermute | solution.py:347
  139.4 111.9 %collective-permute-start.3 = (bf16[384,2048]{1,0:T(8,128)(2,1)S(1)}, bf16[384,2048]{1,0:T(8,128)(2,1)S(1)}, u32[]{:S(2)}, u32[]{:S(2)}) collective-permute-start(bf16[384,2048]{1,0:T(8,128)(2,1)S(1)} %bitcast.8), channel_id=1, source_target_pairs={{0,8},{4,12},{8,0},{12,4},{16,24},{20,28},{24,16},{28,20},{1,9},{5... | collective-permute-start | bytes 4718600 | tf_op jit(solution)/shard_map/ppermute | solution.py:347
  141.4 109.9 %collective-permute-start.2 = (bf16[5,48,2048]{2,1,0:T(8,128)(2,1)}, bf16[5,48,2048]{2,1,0:T(8,128)(2,1)S(1)}, u32[]{:S(2)}, u32[]{:S(2)}) collective-permute-start(bf16[5,48,2048]{2,1,0:T(8,128)(2,1)} %get-tuple-element.66), channel_id=1, source_target_pairs={{0,8},{4,12},{8,0},{12,4},{16,24},{20,28},{24,16},{28,20},{1,9},{5... | collective-permute-start | bytes 2949128 | tf_op jit(solution)/shard_map/ppermute | solution.py:347
  141.4 109.8 %collective-permute-start.1 = (bf16[5,48,2048]{2,1,0:T(8,128)(2,1)S(1)}, bf16[5,48,2048]{2,1,0:T(8,128)(2,1)S(1)}, u32[]{:S(2)}, u32[]{:S(2)}) collective-permute-start(bf16[5,48,2048]{2,1,0:T(8,128)(2,1)S(1)} %copy-done.22), channel_id=1, source_target_pairs={{0,16},{4,20},{8,24},{12,28},{16,0},{20,4},{24,8},{28,12},{1,17},{... | collective-permute-start | bytes 2949128 | tf_op jit(solution)/shard_map/ppermute | solution.py:347
  251.2 144.1 %copy-start.5 = (bf16[5,48,2048]{2,1,0:T(8,128)(2,1)}, bf16[5,48,2048]{2,1,0:T(8,128)(2,1)S(1)}, u32[]{:S(2)}) copy-start(bf16[5,48,2048]{2,1,0:T(8,128)(2,1)S(1)} %collective-permute-done.2.refs_2_) | copy-start | bytes 2949124
  251.2 144.1 %copy-start.7 = (bf16[5,48,2048]{2,1,0:T(8,128)(2,1)}, bf16[5,48,2048]{2,1,0:T(8,128)(2,1)S(1)}, u32[]{:S(2)}) copy-start(bf16[5,48,2048]{2,1,0:T(8,128)(2,1)S(1)} %collective-permute-done.1.refs_4_) | copy-start | bytes 2949124
  253.6 44.0 %collective-permute-start.5 = (bf16[5,48,2048]{2,1,0:T(8,128)(2,1)}, bf16[5,48,2048]{2,1,0:T(8,128)(2,1)}, u32[]{:S(2)}, u32[]{:S(2)}) collective-permute-start(bf16[5,48,2048]{2,1,0:T(8,128)(2,1)} %get-tuple-element.70), channel_id=1, source_target_pairs={{0,4},{4,0},{8,12},{12,8},{16,20},{20,16},{24,28},{28,24},{1,5},{5... | collective-permute-start | bytes 2949128 | tf_op jit(solution)/shard_map/ppermute | solution.py:347
  254.1 43.5 %copy-start.35 = (bf16[384,2048]{1,0:T(8,128)(2,1)S(1)}, bf16[384,2048]{1,0:T(8,128)(2,1)}, u32[]{:S(2)}) copy-start(bf16[384,2048]{1,0:T(8,128)(2,1)} %copy-done.34) | copy-start | bytes 4718596
  254.1 77.7 %collective-permute-start.6 = (bf16[384,2048]{1,0:T(8,128)(2,1)}, bf16[384,2048]{1,0:T(8,128)(2,1)S(1)}, u32[]{:S(2)}, u32[]{:S(2)}) collective-permute-start(bf16[384,2048]{1,0:T(8,128)(2,1)} %copy-done.32), channel_id=1, source_target_pairs={{0,8},{4,12},{8,0},{12,4},{16,24},{20,28},{24,16},{28,20},{1,9},{5... | collective-permute-start | bytes 4718600 | tf_op jit(solution)/shard_map/ppermute | solution.py:347
  255.3 56.3 %collective-permute-start.7 = (bf16[5,48,2048]{2,1,0:T(8,128)(2,1)}, bf16[5,48,2048]{2,1,0:T(8,128)(2,1)S(1)}, u32[]{:S(2)}, u32[]{:S(2)}) collective-permute-start(bf16[5,48,2048]{2,1,0:T(8,128)(2,1)} %copy-done.20), channel_id=1, source_target_pairs={{0,20},{4,16},{8,28},{12,24},{16,4},{20,0},{24,12},{28,8},{1,21},{... | collective-permute-start | bytes 2949128 | tf_op jit(solution)/shard_map/ppermute | solution.py:347
  257.1 74.7 %collective-permute-start.8 = (bf16[5,48,2048]{2,1,0:T(8,128)(2,1)}, bf16[5,48,2048]{2,1,0:T(8,128)(2,1)S(1)}, u32[]{:S(2)}, u32[]{:S(2)}) collective-permute-start(bf16[5,48,2048]{2,1,0:T(8,128)(2,1)} %get-tuple-element.76), channel_id=1, source_target_pairs={{0,28},{4,24},{8,20},{12,16},{16,12},{20,8},{24,4},{28,0},{1,29},{... | collective-permute-start | bytes 2949128 | tf_op jit(solution)/shard_map/ppermute | solution.py:347
  301.4 34.2 %copy-start.23 = (bf16[384,2048]{1,0:T(8,128)(2,1)}, bf16[384,2048]{1,0:T(8,128)(2,1)S(1)}, u32[]{:S(2)}) copy-start(bf16[384,2048]{1,0:T(8,128)(2,1)S(1)} %convolution_convert_fusion.3) | copy-start | bytes 4718596
  309.3 26.3 %copy-start.28 = (bf16[384,2048]{1,0:T(8,128)(2,1)}, bf16[384,2048]{1,0:T(8,128)(2,1)S(1)}, u32[]{:S(2)}) copy-start(bf16[384,2048]{1,0:T(8,128)(2,1)S(1)} %convolution_convert_fusion) | copy-start | bytes 4718596
  310.9 26.5 %collective-permute-start.10 = (bf16[384,2048]{1,0:T(8,128)(2,1)}, bf16[384,2048]{1,0:T(8,128)(2,1)}, u32[]{:S(2)}, u32[]{:S(2)}) collective-permute-start(bf16[384,2048]{1,0:T(8,128)(2,1)} %broadcast_select_fusion.2), channel_id=1, source_target_pairs={{0,1},{1,0},{2,3},{3,2},{4,5},{5,4},{6,7},{7,6},{8,9},{9,8},{10,11... | collective-permute-start | bytes 4718600 | tf_op jit(solution)/shard_map/ppermute | solution.py:350
  311.6 24.1 %copy-start.9 = (bf16[5,48,2048]{2,1,0:T(8,128)(2,1)}, bf16[5,48,2048]{2,1,0:T(8,128)(2,1)S(1)}, u32[]{:S(2)}) copy-start(bf16[5,48,2048]{2,1,0:T(8,128)(2,1)S(1)} %collective-permute-done.7.refs_5_) | copy-start | bytes 2949124
  337.3 3.8 collective-permute-start.9
  344.2 51.1 %copy-start.10 = (bf16[5,48,2048]{2,1,0:T(8,128)(2,1)S(1)}, bf16[5,48,2048]{2,1,0:T(8,128)(2,1)}, u32[]{:S(2)}) copy-start(bf16[5,48,2048]{2,1,0:T(8,128)(2,1)} %copy-done.9) | copy-start | bytes 2949124
  344.2 19.6 %collective-permute-start.13 = (bf16[192,2048]{1,0:T(8,128)(2,1)S(1)}, bf16[192,2048]{1,0:T(8,128)(2,1)S(1)}, u32[]{:S(2)}, u32[]{:S(2)}) collective-permute-start(bf16[192,2048]{1,0:T(8,128)(2,1)S(1)} %get-tuple-element.91), channel_id=1, source_target_pairs={{0,2},{1,3},{2,0},{3,1},{4,6},{5,7},{6,4},{7,5},{8,10},{9,11},{10,... | collective-permute-start | bytes 2359304 | tf_op jit(solution)/shard_map/ppermute | solution.py:350
  345.8 26.5 %collective-permute-start.12 = (bf16[5,48,2048]{2,1,0:T(8,128)(2,1)S(1)}, bf16[5,48,2048]{2,1,0:T(8,128)(2,1)S(1)}, u32[]{:S(2)}, u32[]{:S(2)}) collective-permute-start(bf16[5,48,2048]{2,1,0:T(8,128)(2,1)S(1)} %copy-done.36), channel_id=1, source_target_pairs={{0,24},{4,28},{8,16},{12,20},{16,8},{20,12},{24,0},{28,4},{1,25},{... | collective-permute-start | bytes 2949128 | tf_op jit(solution)/shard_map/ppermute | solution.py:347
  348.8 44.5 %collective-permute-start.11 = (bf16[5,48,2048]{2,1,0:T(8,128)(2,1)S(1)}, bf16[5,48,2048]{2,1,0:T(8,128)(2,1)S(1)}, u32[]{:S(2)}, u32[]{:S(2)}) collective-permute-start(bf16[5,48,2048]{2,1,0:T(8,128)(2,1)S(1)} %copy-done.19), channel_id=1, source_target_pairs={{0,12},{4,8},{8,4},{12,0},{16,28},{20,24},{24,20},{28,16},{1,13},{... | collective-permute-start | bytes 2949128 | tf_op jit(solution)/shard_map/ppermute | solution.py:347
  363.9 29.4 %collective-permute-start.15 = (bf16[192,2048]{1,0:T(8,128)(2,1)S(1)}, bf16[192,2048]{1,0:T(8,128)(2,1)S(1)}, u32[]{:S(2)}, u32[]{:S(2)}) collective-permute-start(bf16[192,2048]{1,0:T(8,128)(2,1)S(1)} %get-tuple-element.92), channel_id=1, source_target_pairs={{0,2},{1,3},{2,0},{3,1},{4,6},{5,7},{6,4},{7,5},{8,10},{9,11},{10,... | collective-permute-start | bytes 2359304 | tf_op jit(solution)/shard_map/ppermute | solution.py:350
  372.3 23.1 %copy-start.30 = (bf16[5,48,2048]{2,1,0:T(8,128)(2,1)}, bf16[5,48,2048]{2,1,0:T(8,128)(2,1)S(1)}, u32[]{:S(2)}) copy-start(bf16[5,48,2048]{2,1,0:T(8,128)(2,1)S(1)} %collective-permute-done.12.refs_6_) | copy-start | bytes 2949124
  393.9 13.5 %collective-permute-start.14 = (bf16[192,2048]{1,0:T(8,128)(2,1)S(1)}, bf16[192,2048]{1,0:T(8,128)(2,1)S(1)}, u32[]{:S(2)}, u32[]{:S(2)}) collective-permute-start(bf16[192,2048]{1,0:T(8,128)(2,1)S(1)} %get-tuple-element.116), channel_id=1, source_target_pairs={{0,0},{1,16},{2,8},{3,24},{4,4},{5,20},{6,12},{7,28},{8,9},{9,25},... | collective-permute-start | bytes 2359304 | tf_op jit(solution)/shard_map/ppermute | solution.py:501
  394.6 12.8 %collective-permute-start.16 = (bf16[192,2048]{1,0:T(8,128)(2,1)S(1)}, bf16[192,2048]{1,0:T(8,128)(2,1)S(1)}, u32[]{:S(2)}, u32[]{:S(2)}) collective-permute-start(bf16[192,2048]{1,0:T(8,128)(2,1)S(1)} %get-tuple-element.115), channel_id=1, source_target_pairs={{0,0},{1,16},{2,8},{3,24},{4,4},{5,20},{6,12},{7,28},{8,9},{9,25},... | collective-permute-start | bytes 2359304 | tf_op jit(solution)/shard_map/ppermute | solution.py:501
  407.5 38.6 %copy-start.31 = (f32[2]{0:T(128)S(1)}, f32[2]{0:T(128)}, u32[]{:S(2)}) copy-start(f32[2]{0:T(128)} %constant.17.clone) | copy-start | bytes 28
  413.6 28.9 %collective-permute-start.17 = (f32[192,2]{1,0:T(8,128)S(1)}, f32[192,2]{1,0:T(8,128)S(1)}, u32[]{:S(2)}, u32[]{:S(2)}) collective-permute-start(f32[192,2]{1,0:T(8,128)S(1)} %shard_map.158), channel_id=1, source_target_pairs={{0,1},{1,0},{2,3},{3,2},{4,5},{5,4},{6,7},{7,6},{8,9},{9,8},{10,11... | collective-permute-start | bytes 4616 | tf_op jit(solution)/shard_map/ppermute | solution.py:350
  438.7 5.8 %collective-permute-start.18 = (f32[192,2]{1,0:T(8,128)S(1)}, f32[192,2]{1,0:T(8,128)S(1)}, u32[]{:S(2)}, u32[]{:S(2)}) collective-permute-start(f32[192,2]{1,0:T(8,128)S(1)} %shard_map.158), channel_id=1, source_target_pairs={{0,2},{1,3},{2,0},{3,1},{4,6},{5,7},{6,4},{7,5},{8,10},{9,11},{10,... | collective-permute-start | bytes 4616 | tf_op jit(solution)/shard_map/ppermute | solution.py:350
  440.9 5.1 %collective-permute-start.19 = (f32[192,2]{1,0:T(8,128)S(1)}, f32[192,2]{1,0:T(8,128)S(1)}, u32[]{:S(2)}, u32[]{:S(2)}) collective-permute-start(f32[192,2]{1,0:T(8,128)S(1)} %shard_map.158), channel_id=1, source_target_pairs={{0,3},{1,2},{2,1},{3,0},{4,7},{5,6},{6,5},{7,4},{8,11},{9,10},{10,... | collective-permute-start | bytes 4616 | tf_op jit(solution)/shard_map/ppermute | solution.py:350
  (26 other events, 73.9 us)
